TPU v7x, 32 devices: a whole 2x2x4 slice. The times are simulated.
32 devices in a mesh: pix: 8 (over z, x), ch: 4 (over y, core).
Axes of the slice: x: 2, y: 2, z: 4, core: 2. Of those that a mesh axis runs over, the one named last changes fastest.
Arguments:
- pixels: bfloat16 [384, 32768], P('pix', 'ch'), may hold values from -6 to 6
- cotangent: bfloat16 [384, 32768], P('pix', 'ch'), may hold values from -6 to 6
- crop_rows: int32 [16], replicated, may hold values from 1 to 32, 384 in all
- condition: bfloat16 [16, 1024], replicated, may hold values from -6 to 6
- context: bfloat16 [16, 4, 1024], replicated, may hold values from -6 to 6
- kernels: bfloat16 [1024, 18432], P('pix', 'ch'), may hold values from -0.0625 to 0.0625
- attention: bfloat16 [1024, 6144], P('pix', 'ch'), as said below
- embedding: bfloat16 [1024, 2048], P('pix', 'ch'), may hold values from -0.1875 to 0.1875
- gains: float32 [3, 1024], P(None, 'ch'), may hold values from 0.1 to 1.9
- shifts: float32 [3, 1024], P(None, 'ch'), may hold values from -2 to 2
- offsets: float32 [4, 1024], P(None, 'ch'), may hold values from -2 to 2
Outputs:
- result: float32 [384, 32768], P('pix', 'ch')
- grad_pixels: float32 [384, 32768], P('pix', 'ch')
- grad_kernels: float32 [1024, 18432], P('pix', 'ch')
- grad_attention: float32 [1024, 6144], P('pix', 'ch')
- grad_embedding: float32 [1024, 2048], P('pix', 'ch')
- grad_gains: float32 [3, 1024], P(None, 'ch')
- grad_shifts: float32 [3, 1024], P(None, 'ch')
- grad_offsets: float32 [4, 1024], P(None, 'ch')
Inputs may be any that keep to these rules, and one draw needn't show every extreme that they name: crop_rows sums to 384; the largest entry is 32. `attention`: drawn as weights scaled by the fan-in of each matrix.
All inputs are finite; a program needn't handle non-finite values.
Results may differ from a plain program's by a relative error of at most 0.025.
Values may be sent and summed in bfloat16 or wider, within the bound.
No kernel may reach another device: no remote copies, remote signals or barrier semaphores. Data moves between devices by JAX's collectives and lax.ppermute only.
A program may use at most 448 MiB of HBM per device.

v0:
```python
import functools

import jax
import jax.numpy as jnp
from jax import lax
from jax.experimental import pallas as pl
from jax.experimental.pallas import tpu as pltpu
from jax.sharding import PartitionSpec as P

HEAD_DIM = 64
W = 32
CROP_ROWS = 32
CTX = 4
GSIZE = 32
HALO = (CROP_ROWS - 1) * W
QB = 256
KB = 256

HIGHEST = lax.Precision.HIGHEST
EPSILON = 1e-05
NEGATIVE = -1e30
BF = jnp.bfloat16
F32 = jnp.float32
VMEM_LIMIT = 58 * 1024 * 1024


def dot(left, right, dims):
    return lax.dot_general(left, right, (dims, ((), ())), preferred_element_type=F32)


NN = ((1,), (0,))
NT = ((1,), (1,))
TN = ((0,), (0,))


def params(**more):
    return pltpu.CompilerParams(vmem_limit_bytes=VMEM_LIMIT, **more)


def cost(flops, moved, exps=0):
    return pl.CostEstimate(flops=flops, bytes_accessed=moved, transcendentals=exps)


WITH_PREV, WITH_NEXT, INVERSE = 3, 4, 5
EDGE = 40


def exact(left, right):
    return lax.dot_general(
        left, right, (NN, ((), ())), precision=HIGHEST, preferred_element_type=F32
    )


def write_totals(first, second, same_ref, totals_ref, next_ref, prev_ref):
    lines, width = first.shape
    row = lax.broadcasted_iota(jnp.int32, (width, width), 0) // GSIZE
    column = lax.broadcasted_iota(jnp.int32, (width, width), 1) // GSIZE
    group = (row == column).astype(F32)
    for place, value in ((0, first), (1, second)):
        total = exact(same_ref[...], exact(value, group))
        totals_ref[place] = total
        next_ref[W + place : W + place + 1, :] = total[lines - 1 : lines, :]
        prev_ref[W + place : W + place + 1, :] = total[0:1, :]
    for target in (next_ref, prev_ref):
        target[W + 2 : EDGE, :] = jnp.zeros((EDGE - W - 2, width), F32)


def crop_means(totals_ref, before_ref, after_ref, rows_ref):
    found = []
    for place in range(2):
        line = slice(W + place, W + place + 1)
        total = totals_ref[place] + rows_ref[WITH_PREV] * before_ref[line, :]
        total = total + rows_ref[WITH_NEXT] * after_ref[line, :]
        found.append(total * rows_ref[INVERSE])
    return found


def square_sums(value_ref, sums_ref):
    lines = sums_ref.shape[1]

    def one(line, carry):
        cells = value_ref[pl.ds(pl.multiple_of(line * W, W), W), :]
        sums_ref[0, pl.ds(line, 1), :] = jnp.sum(cells, axis=0, keepdims=True)
        sums_ref[1, pl.ds(line, 1), :] = jnp.sum(cells * cells, axis=0, keepdims=True)
        return carry

    lax.fori_loop(0, lines, one, 0, unroll=4)


def stats_shapes(lines, width):
    return (
        jax.ShapeDtypeStruct((2, lines, width), F32),
        jax.ShapeDtypeStruct((EDGE, width), F32),
        jax.ShapeDtypeStruct((EDGE, width), F32),
    )


def stats_body(value_ref, same_ref, totals_ref, next_ref, prev_ref, sums_ref):
    tokens = value_ref.shape[0]
    square_sums(value_ref, sums_ref)
    write_totals(sums_ref[0], sums_ref[1], same_ref, totals_ref, next_ref, prev_ref)
    next_ref[0:W, :] = value_ref[tokens - W :, :]
    prev_ref[0:W, :] = value_ref[0:W, :]


def stats(value, same):
    tokens, width = value.shape
    return pl.pallas_call(
        stats_body,
        out_shape=stats_shapes(tokens // W, width),
        scratch_shapes=[pltpu.VMEM((2, tokens // W, width), F32)],
        compiler_params=params(),
        cost_estimate=cost(tokens * width * 4, tokens * width * 4),
        name="stats",
    )(value, same)


def norm_body(active, wide, *refs):
    value_ref, totals_ref, before_ref, after_ref, rows_ref, gain_ref, shift_ref = refs[:7]
    refs = refs[7:]
    if active == "mixed":
        growth_ref, add_ref = refs[:2]
        refs = refs[2:]
    out_ref, stats_ref, scale_ref, bias_ref = refs
    lines = totals_ref.shape[1]
    mean, square = crop_means(totals_ref, before_ref, after_ref, rows_ref)
    scale = lax.rsqrt(square - mean * mean + EPSILON)
    stats_ref[0] = mean
    stats_ref[1] = scale
    if active == "mixed":
        scale_ref[...] = scale * gain_ref[...] * growth_ref[...]
        bias_ref[...] = shift_ref[...] * growth_ref[...] + add_ref[...]
    else:
        scale_ref[...] = scale * gain_ref[...]
        bias_ref[...] = jnp.broadcast_to(shift_ref[...], bias_ref.shape)

    def cells_of(cells, line):
        here = pl.ds(line, 1)
        value = (cells - stats_ref[0, here, :]) * scale_ref[here, :] + bias_ref[here, :]
        if active is not None:
            value = value / (1.0 + jnp.exp(-value))
        return value.astype(BF)

    base = W if wide else 0

    def one(line, carry):
        start = pl.multiple_of(line * W, W)
        out_ref[pl.ds(start + base, W), :] = cells_of(value_ref[pl.ds(start, W), :], line)
        return carry

    lax.fori_loop(0, lines, one, 0, unroll=4)
    if wide:
        out_ref[0:W, :] = cells_of(before_ref[0:W, :], 0)
        out_ref[(lines + 1) * W :, :] = cells_of(after_ref[0:W, :], lines - 1)


def norm(value, totals, before, after, rows, gain, shift, mixed=None, active="plain", wide=True):
    tokens, width = value.shape
    lines = tokens // W
    operands = [value, totals, before, after, rows, gain, shift]
    if mixed is not None:
        operands += list(mixed)
        active = "mixed"
    return pl.pallas_call(
        functools.partial(norm_body, active, wide),
        out_shape=(
            jax.ShapeDtypeStruct((tokens + (2 * W if wide else 0), width), BF),
            jax.ShapeDtypeStruct((2, lines, width), F32),
        ),
        scratch_shapes=[pltpu.VMEM((lines, width), F32), pltpu.VMEM((lines, width), F32)],
        compiler_params=params(),
        cost_estimate=cost(tokens * width * 12, tokens * width * 6, tokens * width),
        name="norm",
    )(*operands)


def sums_body(count, active, *refs):
    parts = refs[:count]
    value_ref, stats_ref, gain_ref, shift_ref, same_ref = refs[count : count + 5]
    refs = refs[count + 5 :]
    if active == "mixed":
        growth_ref, add_ref = refs[:2]
        refs = refs[2:]
    grad_ref, raw_ref, totals_ref, next_ref, prev_ref = refs
    tokens, width = value_ref.shape
    lines = tokens // W

    def one(line, carry):
        here = pl.ds(line, 1)
        cells = pl.ds(pl.multiple_of(line * W, W), W)
        grad = parts[0][cells, :].astype(F32)
        for part in parts[1:]:
            grad = grad + part[cells, :].astype(F32)
        normal = (value_ref[cells, :] - stats_ref[0, here, :]) * stats_ref[1, here, :]
        if active is not None:
            inner = normal * gain_ref[...] + shift_ref[...]
            if active == "mixed":
                inner = inner * growth_ref[here, :] + add_ref[here, :]
            sigmoid = 1.0 / (1.0 + jnp.exp(-inner))
            grad = grad * sigmoid * (1.0 + inner * (1.0 - sigmoid))
        raw_ref[0, here, :] = jnp.sum(grad, axis=0, keepdims=True)
        raw_ref[1, here, :] = jnp.sum(grad * normal, axis=0, keepdims=True)
        if active == "mixed":
            grad = grad * growth_ref[here, :]
        grad_ref[cells, :] = grad
        return carry

    lax.fori_loop(0, lines, one, 0, unroll=4)
    first, second = raw_ref[0] * gain_ref[...], raw_ref[1] * gain_ref[...]
    if active == "mixed":
        first, second = first * growth_ref[...], second * growth_ref[...]
    write_totals(first, second, same_ref, totals_ref, next_ref, prev_ref)
    next_ref[0:W, :] = grad_ref[tokens - W :, :]
    prev_ref[0:W, :] = grad_ref[0:W, :]


def gradient_sums(parts, value, stats_found, gain, shift, same, mixed=None, active=None):
    tokens, width = value.shape
    operands = [*parts, value, stats_found, gain, shift, same]
    if mixed is not None:
        operands += list(mixed)
        active = "mixed"
    return pl.pallas_call(
        functools.partial(sums_body, len(parts), active),
        out_shape=(
            jax.ShapeDtypeStruct((tokens, width), F32),
            jax.ShapeDtypeStruct((2, tokens // W, width), F32),
        )
        + stats_shapes(tokens // W, width),
        compiler_params=params(),
        cost_estimate=cost(tokens * width * 20, tokens * width * 14, tokens * width),
        name="gradient_sums",
    )(*operands)


def norm_gradient(grad, value, line, stats_ref, mean_ref, gain_ref):
    here = pl.ds(line, 1)
    scale = stats_ref[1, here, :]
    normal = (value - stats_ref[0, here, :]) * scale
    return scale * (grad * gain_ref[...] - mean_ref[0, here, :] - normal * mean_ref[1, here, :])


def write_taps(wide_ref, rows_ref, taps_ref):
    tokens = taps_ref.shape[0]
    width = wide_ref.shape[1]
    column = lax.broadcasted_iota(jnp.int32, (W, width), 0)

    def spread_row(line, carry):
        start = pl.multiple_of(line * W, W)
        target = pl.ds(start, W)
        for up in range(3):
            mask = rows_ref[up, pl.ds(line, 1), :]
            values = wide_ref[pl.ds(start + up * W, W), :].astype(F32) * mask
            left = jnp.where(column > 0, pltpu.roll(values, 1, 0), 0.0)
            right = jnp.where(column < W - 1, pltpu.roll(values, W - 1, 0), 0.0)
            for side, moved in enumerate((left, values, right)):
                tap = 8 - (3 * up + side)
                taps_ref[target, tap * width : (tap + 1) * width] = moved.astype(BF)
        return carry

    lax.fori_loop(0, tokens // W, spread_row, 0, unroll=2)


def taps_body(based, ids, *refs):
    grad_ref, value_ref, value_before, value_after, stats_ref, totals_ref = refs[:6]
    before_ref, after_ref, rows_ref, gain_ref = refs[6:10]
    refs = refs[10:]
    if based:
        base_ref, base_before, base_after = refs[:3]
        refs = refs[3:]
    map_ref = refs[0]
    refs = refs[1:]
    if based:
        full_ref = refs[0]
        refs = refs[1:]
    taps_ref = refs[0]
    refs = refs[1:]
    low_ref, same_core, other_core, wide_ref, mean_ref = refs
    tokens, width = grad_ref.shape
    lines = tokens // W
    padded = tokens + 2 * W

    @pl.when(pl.program_id(0) == 0)
    def _():
        mean_ref[0], mean_ref[1] = crop_means(totals_ref, before_ref, after_ref, rows_ref)

        def one(line, carry):
            start = pl.multiple_of(line * W, W)
            cells = pl.ds(start, W)
            found = norm_gradient(
                grad_ref[cells, :], value_ref[cells, :], line, stats_ref, mean_ref, gain_ref
            )
            if based:
                found = found + base_ref[cells, :].astype(F32)
                full_ref[cells, :] = found
            wide_ref[pl.ds(start + W, W), :] = found
            return carry

        lax.fori_loop(0, lines, one, 0, unroll=4)
        for edge_ref, edge_value, line, start in (
            (before_ref, value_before, 0, 0),
            (after_ref, value_after, lines - 1, padded - W),
        ):
            found = norm_gradient(
                edge_ref[0:W, :], edge_value[0:W, :], line, stats_ref, mean_ref, gain_ref
            )
            if based:
                found = found + (base_before if line == 0 else base_after)[0:W, :].astype(F32)
            wide_ref[start : start + W, :] = found

        write_taps(wide_ref, rows_ref, taps_ref)
        low_ref[...] = wide_ref[...].astype(BF)

    core = ids[ids.shape[0] - 1]
    write_products(taps_ref, map_ref, core, same_core, other_core)


def write_products(grad_ref, map_ref, core, same_core, other_core):
    tokens, width = same_core.shape[1:]
    for place, target in ((core, same_core), (1 - core, other_core)):
        rows = pl.ds(pl.multiple_of(place * width, width), width)
        for start in range(0, tokens, 512):
            here = slice(start, start + 512)
            target[0, here, :] = dot(grad_ref[here, :], map_ref[rows, :], NT).astype(BF)


def gradient_taps(
    grad, value, beside, stats_found, totals, before, after, rows, gain, base, ids, maps
):
    tokens, width = grad.shape
    lines = tokens // W
    count = ids.shape[0] - 1
    wide = 9 * width
    operands = [grad, value, *beside, stats_found, totals, before, after, rows, gain]
    if base is not None:
        operands += list(base)
    whole = lambda array: pl.BlockSpec(array.shape, lambda step, ids: (0,) * len(array.shape))
    in_specs = [whole(operand) for operand in operands]
    operands.append(maps)
    in_specs.append(pl.BlockSpec((2 * width, wide), lambda step, ids: (ids[step], 0)))
    taps_shape = jax.ShapeDtypeStruct((tokens, wide), BF)
    shapes, out_specs = [taps_shape], [whole(taps_shape)]
    if base is not None:
        full_shape = jax.ShapeDtypeStruct((tokens, width), F32)
        shapes, out_specs = [full_shape] + shapes, [whole(full_shape)] + out_specs
    low_shape = jax.ShapeDtypeStruct((tokens + 2 * W, width), BF)
    shapes.append(low_shape)
    out_specs.append(whole(low_shape))
    shapes += [jax.ShapeDtypeStruct((count, tokens, width), BF)] * 2
    out_specs += [pl.BlockSpec((1, tokens, width), lambda step, ids: (step, 0, 0))] * 2
    return pl.pallas_call(
        functools.partial(taps_body, base is not None),
        out_shape=shapes,
        grid_spec=pltpu.PrefetchScalarGridSpec(
            num_scalar_prefetch=1,
            grid=(count,),
            in_specs=in_specs,
            out_specs=out_specs,
            scratch_shapes=[
                pltpu.VMEM((tokens + 2 * W, width), F32),
                pltpu.VMEM((2, lines, width), F32),
            ],
        ),
        compiler_params=params(),
        cost_estimate=cost(2 * tokens * count * width * wide, tokens * wide * 4),
        name="gradient_taps",
    )(ids, *operands)


def last_body(grad_ref, value_ref, stats_ref, totals_ref, before_ref, after_ref, rows_ref, gain_ref,
              base_ref, out_ref, mean_ref):
    mean_ref[0], mean_ref[1] = crop_means(totals_ref, before_ref, after_ref, rows_ref)

    def one(line, carry):
        cells = pl.ds(pl.multiple_of(line * W, W), W)
        out_ref[cells, :] = base_ref[cells, :] + norm_gradient(
            grad_ref[cells, :], value_ref[cells, :], line, stats_ref, mean_ref, gain_ref
        )
        return carry

    lax.fori_loop(0, grad_ref.shape[0] // W, one, 0, unroll=4)


def last_gradient(grad, value, stats_found, totals, before, after, rows, gain, base):
    tokens, width = grad.shape
    return pl.pallas_call(
        last_body,
        out_shape=jax.ShapeDtypeStruct((tokens, width), F32),
        scratch_shapes=[pltpu.VMEM((2, tokens // W, width), F32)],
        compiler_params=params(),
        cost_estimate=cost(tokens * width * 10, tokens * width * 16),
        name="last_gradient",
    )(grad, value, stats_found, totals, before, after, rows, gain, base)


def conv_body(count, resid, ids, *refs):
    blocks = refs[:count]
    kernel_ref, rows_ref = refs[count : count + 2]
    refs = refs[count + 2 :]
    if resid:
        input_ref, bias_ref = refs[:2]
        refs = refs[2:]
    same_ref, out_ref, totals_ref, next_ref, prev_ref, all_ref, sums_ref = refs
    tokens, width = out_ref.shape
    for place in range(count):
        lanes = pl.ds(pl.multiple_of(ids[place] * width, width), width)
        all_ref[:, lanes] = blocks[place][...]
    chunk = 256
    lines = chunk // W
    for start in range(0, tokens, chunk):
        here = slice(start, start + chunk)
        sides = [None] * 3
        for up in range(3):
            taps = kernel_ref[:, up * 3 * width : (up + 1) * 3 * width]
            part = dot(all_ref[up * W + start : up * W + start + chunk, :], taps, NN)
            part = part.reshape(lines, W, 3 * width)
            mask = rows_ref[up, start // W : start // W + lines, :][:, None, :]
            for side in range(3):
                piece = part[:, :, side * width : (side + 1) * width]
                piece = piece if up == 1 else piece * mask
                sides[side] = piece if sides[side] is None else sides[side] + piece
        sides = [piece.reshape(chunk, width) for piece in sides]
        column = lax.broadcasted_iota(jnp.int32, (chunk, width), 0) % W
        left = jnp.where(column > 0, pltpu.roll(sides[0], 1, 0), 0.0)
        right = jnp.where(column < W - 1, pltpu.roll(sides[2], chunk - 1, 0), 0.0)
        total = sides[1] + left + right
        if resid:
            total += input_ref[here, :] + bias_ref[...]
        out_ref[here, :] = total
    square_sums(out_ref, sums_ref)
    write_totals(sums_ref[0], sums_ref[1], same_ref, totals_ref, next_ref, prev_ref)
    next_ref[0:W, :] = out_ref[tokens - W :, :]
    prev_ref[0:W, :] = out_ref[0:W, :]


def convolve(blocks, ids, kernel, rows, same, resid):
    count = len(blocks)
    padded, width = blocks[0].shape
    tokens = padded - 2 * W
    lines = tokens // W
    operands = [*blocks, kernel, rows, *resid, same]

    def whole(array):
        return pl.BlockSpec(array.shape, lambda step, ids: (0,) * len(array.shape))

    shapes = (jax.ShapeDtypeStruct((tokens, width), F32),) + stats_shapes(lines, width)
    return pl.pallas_call(
        functools.partial(conv_body, count, len(resid)),
        out_shape=shapes,
        grid_spec=pltpu.PrefetchScalarGridSpec(
            num_scalar_prefetch=1,
            grid=(1,),
            in_specs=[whole(operand) for operand in operands],
            out_specs=[whole(shape) for shape in shapes],
            scratch_shapes=[
                pltpu.VMEM((padded, count * width), BF),
                pltpu.VMEM((2, lines, width), F32),
            ],
        ),
        compiler_params=params(),
        cost_estimate=cost(
            18 * tokens * count * width * width, 18 * count * width * width + tokens * width * 12
        ),
        name="convolve",
    )(ids, *operands)


def project_body(count, width, ids, *refs):
    blocks = refs[:count]
    map_ref, out_ref, *edges, all_ref = refs[count:]

    @pl.when(pl.program_id(0) == 0)
    def _():
        for place in range(count):
            first = pl.multiple_of(ids[place] * width, width)
            all_ref[:, pl.ds(first, width)] = blocks[place][...]

    for start in range(0, out_ref.shape[0], 512):
        here = slice(start, start + 512)
        out_ref[here, :] = dot(all_ref[here, :], map_ref[...], NN).astype(out_ref.dtype)
    if edges:
        edges[0][...] = out_ref[0:HALO, :]
        edges[1][...] = out_ref[out_ref.shape[0] - HALO :, :]


def project(blocks, ids, maps, first, wide, edges=False):
    count = len(blocks)
    tokens, width = blocks[0].shape
    depth = maps.shape[0]
    start = first // width
    out_shape = [jax.ShapeDtypeStruct((tokens, wide), BF)]
    out_specs = [pl.BlockSpec((tokens, width), lambda step, ids: (0, step))]
    if edges:
        edge_spec = pl.BlockSpec((HALO, width), lambda step, ids: (0, jnp.maximum(step - 1, 0)))
        out_shape += [jax.ShapeDtypeStruct((HALO, wide - width), BF)] * 2
        out_specs += [edge_spec] * 2
    found = pl.pallas_call(
        functools.partial(project_body, count, width),
        out_shape=out_shape,
        grid_spec=pltpu.PrefetchScalarGridSpec(
            num_scalar_prefetch=1,
            grid=(wide // width,),
            in_specs=[pl.BlockSpec((tokens, width), lambda step, ids: (0, 0))] * count
            + [pl.BlockSpec((depth, width), lambda step, ids: (0, start + step))],
            out_specs=out_specs,
            scratch_shapes=[pltpu.VMEM((tokens, depth), BF)],
        ),
        compiler_params=params(),
        cost_estimate=cost(2 * tokens * depth * wide, (tokens + depth) * wide * 2),
        name="project",
    )(ids, *blocks, maps)
    return found if edges else found[0]


def spread_body(ids, grad_ref, *refs):
    core = ids[ids.shape[0] - 1]
    write_products(grad_ref, refs[0], core, *refs[1:])


def spread(grad, ids, maps, first=0):
    tokens, wide = grad.shape
    count = ids.shape[0] - 1
    width = maps.shape[0] // lax.axis_size("ch")
    start = first // wide
    return pl.pallas_call(
        spread_body,
        out_shape=[jax.ShapeDtypeStruct((count, tokens, width), BF)] * 2,
        grid_spec=pltpu.PrefetchScalarGridSpec(
            num_scalar_prefetch=1,
            grid=(count,),
            in_specs=[
                pl.BlockSpec((tokens, wide), lambda step, ids: (0, 0)),
                pl.BlockSpec((2 * width, wide), lambda step, ids: (ids[step], start)),
            ],
            out_specs=[pl.BlockSpec((1, tokens, width), lambda step, ids: (step, 0, 0))] * 2,
        ),
        compiler_params=params(),
        cost_estimate=cost(4 * tokens * count * width * wide, (tokens + count * width) * wide * 2),
        name="spread",
    )(ids, grad, maps)


def home_body(count, halved, shift, ids, *refs):
    grad_ref, map_ref = refs[:2]
    blocks = refs[2 : 2 + count]
    same_core, other_core, out_ref, turned_ref = refs[2 + count :]
    tokens = grad_ref.shape[0]
    width = blocks[0].shape[1]
    share = width // 2 if halved else width
    write_products(grad_ref, map_ref, ids[1], same_core, other_core)
    for place in range(count):
        rows = pl.ds(pl.multiple_of(ids[3 + place] * share, share), share)
        lanes = slice(None)
        if halved:
            lanes = pl.ds(pl.multiple_of(ids[2] * share, share), share)
        turned_ref[rows, :] = blocks[place][shift : shift + tokens, lanes].T
    depth, wide = out_ref.shape
    for start in range(0, wide, 3 * width):
        columns = slice(start, start + 3 * width)
        out_ref[:, columns] = dot(turned_ref[...], grad_ref[:, columns], NN).astype(out_ref.dtype)


def home_and_outer(grad, ids, maps, blocks, halved=False, first=0, shift=0):
    count = len(blocks)
    tokens, wide = grad.shape
    width = blocks[0].shape[1]
    depth = count * width // (2 if halved else 1)
    start = first // wide
    part = jax.ShapeDtypeStruct((1, tokens, width), BF)

    def whole(array):
        return pl.BlockSpec(array.shape, lambda step, ids: (0,) * len(array.shape))

    result = jax.ShapeDtypeStruct((depth, wide), F32 if halved else BF)
    return pl.pallas_call(
        functools.partial(home_body, count, halved, shift),
        out_shape=[part, part, result],
        grid_spec=pltpu.PrefetchScalarGridSpec(
            num_scalar_prefetch=1,
            grid=(1,),
            in_specs=[
                whole(grad), pl.BlockSpec((2 * width, wide), lambda step, ids: (ids[0], start)),
            ]
            + [whole(block) for block in blocks],
            out_specs=[whole(part), whole(part), whole(result)],
            scratch_shapes=[pltpu.VMEM((depth, tokens), BF)],
        ),
        compiler_params=params(),
        cost_estimate=cost(
            2 * tokens * (depth + 2 * width) * wide, (tokens + depth + 2 * width) * wide * 2
        ),
        name="home_and_outer",
    )(ids, grad, maps, *blocks)


def half_beside_body(count, ids, *refs):
    pairs = refs[:2]
    wide_ref, rows_ref, own_ref, out_ref, turned_ref, taps_ref = refs[2:]
    tokens = taps_ref.shape[0]
    half = pairs[0].shape[1] // (count // 2)
    tile = out_ref.shape[1]
    step = pl.program_id(0)

    @pl.when(step == 0)
    def _():
        write_taps(wide_ref, rows_ref, taps_ref)
        for place in range(count):
            rows = pl.ds(pl.multiple_of(ids[1 + place] * half, half), half)
            lanes = slice(place // 2 * half, (place // 2 + 1) * half)
            turned_ref[rows, :] = pairs[place % 2][:, lanes].T

    columns = pl.ds(pl.multiple_of(step * tile, tile), tile)
    out_ref[...] = (own_ref[...] + dot(turned_ref[...], taps_ref[:, columns], NN)).astype(BF)


def half_beside(pairs, ids, wide_grad, row_masks, own):
    count = ids.shape[0] - 1
    tokens, both = pairs[0].shape
    depth, wide = own.shape
    padded, width = wide_grad.shape
    tile = 3 * width
    once = lambda step, ids: (0, 0)
    return pl.pallas_call(
        functools.partial(half_beside_body, count),
        out_shape=jax.ShapeDtypeStruct((depth, wide), BF),
        grid_spec=pltpu.PrefetchScalarGridSpec(
            num_scalar_prefetch=1,
            grid=(wide // tile,),
            in_specs=[
                pl.BlockSpec((tokens, both), once),
                pl.BlockSpec((tokens, both), once),
                pl.BlockSpec((padded, width), once),
                pl.BlockSpec(row_masks.shape, lambda step, ids: (0, 0, 0)),
                pl.BlockSpec((depth, tile), lambda step, ids: (0, step)),
            ],
            out_specs=pl.BlockSpec((depth, tile), lambda step, ids: (0, step)),
            scratch_shapes=[pltpu.VMEM((depth, tokens), BF), pltpu.VMEM((tokens, wide), BF)],
        ),
        compiler_params=params(),
        cost_estimate=cost(2 * tokens * depth * wide, (tokens + 3 * depth) * wide * 2),
        name="half_beside",
    )(ids, *pairs, wide_grad, row_masks, own)


def outer_body(count, shift, ids, *refs):
    blocks = refs[:count]
    grad_ref, out_ref, turned_ref = refs[count:]
    tokens = grad_ref.shape[0]
    width = blocks[0].shape[1]

    @pl.when(pl.program_id(0) == 0)
    def _():
        for place in range(count):
            first = pl.multiple_of(ids[place] * width, width)
            turned_ref[pl.ds(first, width), :] = blocks[place][shift : shift + tokens, :].T

    depth = turned_ref.shape[0]
    for start in range(0, depth, 512):
        here = slice(start, start + 512)
        out_ref[here, :] = dot(turned_ref[here, :], grad_ref[...], NN).astype(BF)


def outer(blocks, ids, grad, shift=0, columns=None):
    count = len(blocks)
    tokens = grad.shape[0]
    first, wide = columns or (0, grad.shape[1])
    padded, width = blocks[0].shape
    depth = count * width
    tile = min(wide, 3 * width)
    before = first // tile
    return pl.pallas_call(
        functools.partial(outer_body, count, shift),
        out_shape=jax.ShapeDtypeStruct((depth, wide), BF),
        grid_spec=pltpu.PrefetchScalarGridSpec(
            num_scalar_prefetch=1,
            grid=(wide // tile,),
            in_specs=[pl.BlockSpec((padded, width), lambda step, ids: (0, 0))] * count
            + [pl.BlockSpec((tokens, tile), lambda step, ids: (0, before + step))],
            out_specs=pl.BlockSpec((depth, tile), lambda step, ids: (0, step)),
            scratch_shapes=[pltpu.VMEM((depth, tokens), BF)],
        ),
        compiler_params=params(),
        cost_estimate=cost(2 * tokens * depth * wide, (tokens + depth) * wide * 2),
        name="outer",
    )(ids, *blocks, grad)


def pack_body(first_ref, second_ref, out_ref, order_ref, sorted_ref):
    depth, wide = first_ref.shape
    width = wide // 9
    size = order_ref.shape[0]
    for start in range(0, size, 128):
        row = start + lax.broadcasted_iota(jnp.int32, (128, size), 0)
        column = lax.broadcasted_iota(jnp.int32, (128, size), 1)
        wanted = (row & 63) * 18 + (row >> 6)
        order_ref[start : start + 128, :] = jnp.where(column == wanted, 1.0, 0.0).astype(BF)
    lane = lax.broadcasted_iota(jnp.int32, (depth, 128), 1)
    for block in range(width // 128):
        for pair in range(9):
            cells = []
            for tap in (2 * pair, 2 * pair + 1):
                source = first_ref if tap < 9 else second_ref
                at = tap % 9 * width + block * 128
                cells.append(source[:, at : at + 128].astype(F32))
            low = jnp.where(lane < 64, cells[0], pltpu.roll(cells[1], 64, 1))
            high = jnp.where(lane < 64, pltpu.roll(cells[0], 64, 1), cells[1])
            here = slice(pair * 128, (pair + 1) * 128)
            for half, value in ((0, low), (1, high)):
                at = (2 * block + half) * depth
                sorted_ref[at : at + depth, here] = value.astype(BF)
    found = dot(sorted_ref[...], order_ref[...], NN)
    for block in range(width // 64):
        out_ref[:, block * size : (block + 1) * size] = found[block * depth : (block + 1) * depth]


def pack_kernels(first, second):
    depth, wide = first.shape
    size = 64 * 18
    return pl.pallas_call(
        pack_body,
        out_shape=jax.ShapeDtypeStruct((depth, 2 * wide), F32),
        scratch_shapes=[
            pltpu.VMEM((size, size), BF),
            pltpu.VMEM((2 * wide // size * depth, size), BF),
        ],
        compiler_params=params(),
        cost_estimate=cost(4 * depth * wide * size, depth * wide * 12),
        name="pack_kernels",
    )(first, second)


def attention_body(
    heads, starts, counts, crops, chips, query_ref, grad_ref, low_ref, own_ref, high_ref, ckey_ref,
    cval_ref, map_ref, qcrop_ref, ccrop_ref, home_same, home_other, away_same, away_other, att_ref, dquery_ref, dlow_ref, down_ref, dhigh_ref, dckey_ref,
    dcval_ref, keys, values, keys_t, values_t, dkeys, dvalues, kcrop_ref, score_ref, prob_ref,
    cscore_ref, cprob_ref, slope_ref, cslope_ref, qt_ref, qn_ref, gt_ref, gn_ref, att_t, dq_t,
):
    step = pl.program_id(0)
    window, width = keys.shape
    tokens = own_ref.shape[0]

    @pl.when(step == 0)
    def _():
        def label(line, carry):
            here = pl.ds(pl.multiple_of(line * W, W), W)
            kcrop_ref[here, :] = jnp.full((W, 128), crops[line], jnp.int32)
            return carry

        lax.fori_loop(0, window // W, label, 0, unroll=2)
        for place, target, turned in ((0, keys, keys_t), (1, values, values_t)):
            part = slice(place * width, (place + 1) * width)
            target[0:HALO, :] = low_ref[:, part]
            shifted = slice((place + 1) * width, (place + 2) * width)
            target[HALO : HALO + tokens, :] = own_ref[:, shifted]
            target[HALO + tokens : 2 * HALO + tokens, :] = high_ref[:, part]
            rest = window - 2 * HALO - tokens
            target[2 * HALO + tokens :, :] = jnp.zeros((rest, width), BF)
            for place in range(0, window, KB):
                turned[:, place : place + KB] = target[place : place + KB, :].T
        dkeys[...] = jnp.zeros_like(dkeys)
        dvalues[...] = jnp.zeros_like(dvalues)
        dckey_ref[...] = jnp.zeros_like(dckey_ref)
        dcval_ref[...] = jnp.zeros_like(dcval_ref)

    first = starts[step]
    blocks = counts[step]
    query = (query_ref[...].astype(F32) * (HEAD_DIM**-0.5)).astype(BF)
    query_t = query.T
    grad_t = grad_ref[...].T
    lane = lax.broadcasted_iota(jnp.int32, (QB, width), 1)
    zero = jnp.zeros((width, QB), BF)
    mine = [slice(head * HEAD_DIM, (head + 1) * HEAD_DIM) for head in range(heads)]
    part = [slice(head * QB, (head + 1) * QB) for head in range(heads)]
    for head in range(heads):
        qt_ref[:, part[head]] = zero
        qt_ref[mine[head], part[head]] = query_t[mine[head], :]
        gt_ref[:, part[head]] = zero
        in_head = (lane >= head * HEAD_DIM) & (lane < (head + 1) * HEAD_DIM)
        qn_ref[part[head], :] = jnp.where(in_head, query, jnp.zeros_like(query))
    crop_row = qcrop_ref[...].reshape(1, QB)
    same_context = jnp.concatenate([ccrop_ref[...]] * (QB // 128), axis=1) == crop_row

    def span(block):
        return pl.ds(pl.multiple_of(first + block * KB, 128), KB)

    def folded(values, combine):
        return combine(values.reshape(-1, 8, QB), axis=0)

    largest = []
    products = dot(ckey_ref[...], qt_ref[...], NN)
    for head in range(heads):
        scores = jnp.where(same_context, products[:, part[head]], NEGATIVE)
        cscore_ref[:, part[head]] = scores
        largest.append(folded(scores, jnp.max))

    def pass_one(block, carry):
        here = span(block)
        same = jnp.concatenate([kcrop_ref[here, :]] * (QB // 128), axis=1) == crop_row
        products = dot(keys[here, :], qt_ref[...], NN)
        out = []
        for head in range(heads):
            scores = jnp.where(same, products[:, part[head]], NEGATIVE)
            score_ref[block, :, part[head]] = scores
            out.append(jnp.maximum(carry[head], folded(scores, jnp.max)))
        return tuple(out)

    largest = lax.fori_loop(0, blocks, pass_one, tuple(largest))
    largest = [jnp.max(value, axis=0, keepdims=True) for value in largest]

    sums = []
    for head in range(heads):
        prob = jnp.exp(cscore_ref[:, part[head]] - largest[head])
        sums.append(folded(prob, jnp.sum))
        low = prob.astype(BF)
        cprob_ref[:, part[head]] = low
        att_t[mine[head], :] = dot(cval_ref[...], low, TN)[mine[head], :]

    def pass_two(block, carry):
        here = span(block)
        out = []
        for head in range(heads):
            prob = jnp.exp(score_ref[block, :, part[head]] - largest[head])
            out.append(carry[head] + folded(prob, jnp.sum))
            low = prob.astype(BF)
            prob_ref[block, :, part[head]] = low
            att_t[mine[head], :] += dot(values_t[mine[head], here], low, NN)
        return tuple(out)

    sums = lax.fori_loop(0, blocks, pass_two, tuple(sums))
    offsets = []
    for head in range(heads):
        inverse = 1.0 / jnp.sum(sums[head], axis=0, keepdims=True)
        attended = att_t[mine[head], :] * inverse
        att_t[mine[head], :] = attended
        scaled = grad_t[mine[head], :].astype(F32) * inverse
        gt_ref[mine[head], part[head]] = scaled.astype(BF)
        offsets.append(jnp.sum(scaled * attended, axis=0, keepdims=True))
        gn_ref[part[head], :] = gt_ref[:, part[head]].T
    attended = att_t[...].T.astype(BF)
    att_ref[...] = attended
    core = chips[chips.shape[0] - 1]
    for chip in range(chips.shape[0] - 1):
        targets = (home_same, home_other) if chip == 0 else (away_same, away_other)
        for place, target in ((core, targets[0]), (1 - core, targets[1])):
            rows = pl.ds(pl.multiple_of((2 * chips[chip] + place) * width, width), width)
            target[max(chip - 1, 0)] = dot(attended, map_ref[rows, :], NT).astype(BF)

    slope = dot(cval_ref[...], gt_ref[...], NN)
    for head in range(heads):
        prob = cprob_ref[:, part[head]].astype(F32)
        dscore = (prob * (slope[:, part[head]] - offsets[head])).astype(BF)
        cslope_ref[:, part[head]] = dscore
        dq_t[mine[head], :] = dot(ckey_ref[...], dscore, TN)[mine[head], :]
    dcval_ref[...] += dot(cprob_ref[...], gn_ref[...], NN)
    dckey_ref[...] += dot(cslope_ref[...], qn_ref[...], NN)

    def pass_three(block, carry):
        here = span(block)
        slope = dot(values[here, :], gt_ref[...], NN)
        for head in range(heads):
            prob = prob_ref[block, :, part[head]].astype(F32)
            dscore = (prob * (slope[:, part[head]] - offsets[head])).astype(BF)
            slope_ref[:, part[head]] = dscore
            dq_t[mine[head], :] += dot(keys_t[mine[head], here], dscore, NN)
        dvalues[here, :] += dot(prob_ref[block], gn_ref[...], NN)
        dkeys[here, :] += dot(slope_ref[...], qn_ref[...], NN)
        return carry

    lax.fori_loop(0, blocks, pass_three, 0)
    dquery_ref[...] = (dq_t[...] * (HEAD_DIM**-0.5)).T.astype(BF)

    @pl.when(step == pl.num_programs(0) - 1)
    def _():
        for place, source in ((0, dkeys), (1, dvalues)):
            part = slice(place * width, (place + 1) * width)
            dlow_ref[:, part] = source[0:HALO, :].astype(BF)
            down_ref[:, part] = source[HALO : HALO + tokens, :]
            dhigh_ref[:, part] = source[HALO + tokens : 2 * HALO + tokens, :].astype(BF)


def attend(qkv, grad, low, high, ckey, cval, maps, chips, tables):
    starts, counts, crops, qcrop, ccrop = tables
    tokens, width = grad.shape
    heads = width // HEAD_DIM
    window = crops.shape[0] * W
    context = ckey.shape[0]
    most = ((QB // W + 2 * (CROP_ROWS - 1)) * W + 127 + KB - 1) // KB
    q_block = pl.BlockSpec((QB, width), lambda step, *_: (step, 0))

    def whole(array):
        return pl.BlockSpec(array.shape, lambda step, *_: (0,) * len(array.shape))

    full = [low, qkv, high, ckey, cval]
    others = chips.shape[0] - 2
    map_spec = pl.BlockSpec((maps.shape[0], width), lambda step, *_: (0, 3))
    part_shapes = [jax.ShapeDtypeStruct((count, tokens, width), BF) for count in (1, 1, others, others)]
    part_specs = [
        pl.BlockSpec((shape.shape[0], QB, width), lambda step, *_: (0, step, 0))
        for shape in part_shapes
    ]
    shapes = (
        jax.ShapeDtypeStruct((tokens, width), BF),
        jax.ShapeDtypeStruct((tokens, width), BF),
        jax.ShapeDtypeStruct((HALO, 2 * width), BF),
        jax.ShapeDtypeStruct((tokens, 2 * width), F32),
        jax.ShapeDtypeStruct((HALO, 2 * width), BF),
        jax.ShapeDtypeStruct((context, width), F32),
        jax.ShapeDtypeStruct((context, width), F32),
    )
    flops = 12 * tokens * 1280 * width
    return pl.pallas_call(
        functools.partial(attention_body, heads),
        out_shape=(*part_shapes, *shapes),
        grid_spec=pltpu.PrefetchScalarGridSpec(
            num_scalar_prefetch=4,
            grid=(tokens // QB,),
            in_specs=[q_block, q_block]
            + [whole(array) for array in full]
            + [map_spec, pl.BlockSpec((1, 1, QB), lambda step, *_: (step, 0, 0)), whole(ccrop)],
            out_specs=[*part_specs, q_block, q_block] + [whole(shape) for shape in shapes[2:]],
            scratch_shapes=[
                pltpu.VMEM((window, width), BF),
                pltpu.VMEM((window, width), BF),
                pltpu.VMEM((width, window), BF),
                pltpu.VMEM((width, window), BF),
                pltpu.VMEM((window, width), F32),
                pltpu.VMEM((window, width), F32),
                pltpu.VMEM((window, 128), jnp.int32),
                pltpu.VMEM((most, KB, heads * QB), F32),
                pltpu.VMEM((most, KB, heads * QB), BF),
                pltpu.VMEM((context, heads * QB), F32),
                pltpu.VMEM((context, heads * QB), BF),
                pltpu.VMEM((KB, heads * QB), BF),
                pltpu.VMEM((context, heads * QB), BF),
                pltpu.VMEM((width, heads * QB), BF),
                pltpu.VMEM((heads * QB, width), BF),
                pltpu.VMEM((width, heads * QB), BF),
                pltpu.VMEM((heads * QB, width), BF),
                pltpu.VMEM((width, QB), F32),
                pltpu.VMEM((width, QB), F32),
            ],
        ),
        compiler_params=params(),
        cost_estimate=cost(flops // 3, 20 * tokens * width, tokens * 1280 * heads),
        name="attend",
    )(starts, counts, crops, chips, qkv, grad, *full, maps, qcrop, ccrop)


def along_pix(value, by):
    size = lax.axis_size("pix")
    return lax.ppermute(value, "pix", [(i, i + by) for i in range(size) if 0 <= i + by < size])


def across_pix(value, bit):
    return lax.ppermute(value, "pix", [(i, i ^ bit) for i in range(lax.axis_size("pix"))])


def pix_sum(value, bit=1):
    while bit < lax.axis_size("pix"):
        value = value + across_pix(value, bit)
        bit *= 2
    return value


def to_mate(value):
    return lax.ppermute(value, "ch", [(i, i ^ 1) for i in range(lax.axis_size("ch"))])


def to_chip(value, by):
    size = lax.axis_size("ch")
    return lax.ppermute(value, "ch", [(i, (i + 2 * by) % size) for i in range(size)])


def gather_rows(value):
    return lax.all_gather(value, "pix", axis=0, tiled=True)


def paired():
    return lax.axis_size("ch") == 4 and lax.axis_size("pix") == 8


def scatter_lines(value):
    size = lax.axis_size("pix")
    lines = [[2 * i + side for i in range(size // 2)] for side in range(2)]
    return lax.psum_scatter(
        value, "pix", scatter_dimension=0, tiled=True, axis_index_groups=lines
    )


def halves_to_send(blocks, side):
    half = blocks[0].shape[1] // 2
    sent = [
        lax.dynamic_slice_in_dim(block[W:-W], (1 - side) * half, half, axis=1)
        for block in blocks[::2]
    ]
    return jnp.concatenate(sent, axis=1)


def scatter_rows(value):
    return lax.psum_scatter(value, "pix", scatter_dimension=0, tiled=True)


def block_ids():
    size = lax.axis_size("ch")
    here = lax.axis_index("ch")
    ids = [here, here ^ 1]
    for by in range(1, size // 2):
        other = lax.rem(here + size - 2 * by, size)
        ids += [other, other ^ 1]
    return jnp.stack(ids).astype(jnp.int32)


def chip_ids():
    size = lax.axis_size("ch")
    here = lax.axis_index("ch")
    chips = [lax.rem(here // 2 + by, size // 2) for by in range(1, size // 2)]
    home = jnp.stack([here // 2, here % 2]).astype(jnp.int32)
    return home, jnp.stack(chips + [here % 2]).astype(jnp.int32)


def tie(*values):
    return lax.optimization_barrier(values)


def far_blocks(value):
    return [to_chip(value, by) for by in range(1, lax.axis_size("ch") // 2)]


def with_mates(blocks):
    found = []
    for block in blocks:
        found += [block, to_mate(block)]
    return found


def gather_blocks(value):
    far = far_blocks(value)
    return [value, to_mate(value)] + with_mates(far)


def chip_sums(parts):
    own, mate = parts
    return [
        (own[i].astype(F32) + to_mate(mate[i]).astype(F32)).astype(BF) for i in range(own.shape[0])
    ]


def sent_sums(sums):
    return [to_chip(piece, by + 1) for by, piece in enumerate(sums)]


def home_parts(parts):
    return [parts[0][0], to_mate(parts[1][0])]


def unpack_rows(packed):
    lines = packed.shape[0]
    width = packed.shape[1] // W
    return packed.reshape(lines, width, W).transpose(0, 2, 1).reshape(lines * W, width)


def pack_rows(cells):
    width = cells.shape[1]
    lines = cells.shape[0] // W
    return cells.reshape(lines, W, width).transpose(0, 2, 1).reshape(lines, width * W)


def small(left, right):
    return jnp.dot(left, right, precision=HIGHEST)


def turned(left, right):
    return lax.dot_general(left, right, (TN, ((), ())), precision=HIGHEST)


def beside_rows(messages):
    to_next, to_prev = messages
    return along_pix(to_next, 1), along_pix(to_prev, -1)


def local(
    pixels,
    cotangent,
    crop_rows,
    condition,
    context,
    kernels,
    attention,
    embedding,
    gains,
    shifts,
    offsets,
):
    lines = pixels.shape[0]
    width = pixels.shape[1] // W
    tokens = lines * W
    depth_here = kernels.shape[0]
    crop_count = crop_rows.shape[0]
    place = lax.axis_index("pix")
    kernel_local = (
        kernels.reshape(depth_here, width, 18).transpose(0, 2, 1).reshape(depth_here, 18 * width)
    )
    maps_local = (
        attention.reshape(depth_here, width, 6).transpose(0, 2, 1).reshape(depth_here, 6 * width)
    )
    kernel_one = gather_rows(kernel_local[:, : 9 * width])
    two_local = kernel_local[:, 9 * width :]
    four = jnp.concatenate([maps_local[:, : 3 * width], maps_local[:, 5 * width :]], axis=1)
    embedding_local = (
        embedding.reshape(depth_here, width, 2).transpose(0, 2, 1).reshape(depth_here, 2 * width)
    )
    context_flat = context.reshape(-1, context.shape[2])
    own_rows = place * depth_here
    context_own = lax.dynamic_slice_in_dim(context_flat, own_rows, depth_here, axis=1)
    condition_own = lax.dynamic_slice_in_dim(condition, own_rows, depth_here, axis=1)
    summed = jnp.concatenate(
        [
            dot(condition_own, embedding_local, NN),
            dot(context_own, maps_local[:, 3 * width : 5 * width], NN),
        ],
        axis=0,
    )
    summed = summed + across_pix(summed, 1)
    bounds = jnp.cumsum(crop_rows)
    line = place * lines + jnp.arange(-(CROP_ROWS - 1), lines + CROP_ROWS - 1, dtype=jnp.int32)
    found = jnp.sum((line[:, None] >= bounds[None, :]).astype(jnp.int32), axis=1)
    crop_wide = jnp.where((line >= 0) & (line < bounds[-1]), found, -1)
    near = crop_wide[CROP_ROWS - 2 : CROP_ROWS + lines]
    crop_row = near[1:-1]
    same = (crop_row[:, None] == crop_row[None, :]).astype(F32)
    member = (crop_row[:, None] == jnp.arange(crop_count)[None, :]).astype(F32)
    sizes = jnp.sum(jnp.where(member > 0, crop_rows[None, :], 0), axis=1)
    rows = jnp.stack(
        [
            (near[:-2] == crop_row).astype(F32),
            jnp.ones((lines,), F32),
            (near[2:] == crop_row).astype(F32),
            (crop_row == near[0]).astype(F32),
            (crop_row == near[-1]).astype(F32),
            1.0 / (sizes * (W * GSIZE)).astype(F32),
        ]
    )
    rows = jnp.broadcast_to(rows[:, :, None], (6, lines, width))
    if paired():
        other = (place ^ 1) * lines + jnp.arange(-1, lines + 1, dtype=jnp.int32)
        found = jnp.sum((other[:, None] >= bounds[None, :]).astype(jnp.int32), axis=1)
        found = jnp.where((other >= 0) & (other < bounds[-1]), found, -1)
        other_rows = jnp.stack(
            [
                (found[:-2] == found[1:-1]).astype(F32),
                jnp.ones((lines,), F32),
                (found[2:] == found[1:-1]).astype(F32),
            ]
        )
        other_rows = jnp.broadcast_to(other_rows[:, :, None], (3, lines, width))
        side = place % 2
    crop_end = jnp.sum(jnp.where(member > 0, bounds[None, :], 0), axis=1)
    crop_start = crop_end - sizes
    base = place * lines - (CROP_ROWS - 1)
    step = QB // W
    window_low = (crop_start[::step] - base) * W
    window_high = (crop_end[step - 1 :: step] - base) * W
    starts = window_low // 128 * 128
    counts = (window_high - starts + KB - 1) // KB
    window = -(-(2 * HALO + tokens + KB) // KB) * KB
    key_crop = jnp.pad(
        crop_wide, (0, window // W - crop_wide.shape[0]), constant_values=-2
    ).astype(jnp.int32)
    context_crop = jnp.broadcast_to(
        jnp.repeat(jnp.arange(crop_count, dtype=jnp.int32), CTX)[:, None], (crop_count * CTX, 128)
    )
    query_crop = jnp.repeat(crop_row, W).reshape(-1, 1, QB)
    tables = (starts.astype(jnp.int32), counts.astype(jnp.int32), key_crop, query_crop, context_crop)

    ids = block_ids()
    home, away = chip_ids()
    near_side = side if paired() else jnp.zeros_like(place)
    home_ids = jnp.concatenate([home, near_side.astype(jnp.int32)[None], ids])
    gain = [gains[i : i + 1] for i in range(3)]
    shift = [shifts[i : i + 1] for i in range(3)]
    inputs = unpack_rows(pixels).astype(F32)
    dy_low = unpack_rows(cotangent)
    dy_beside = along_pix(dy_low[-W:], 1), along_pix(dy_low[:W], -1)
    totals, *messages = stats(inputs, same)
    messages, summed = tie(messages, summed)
    summed = summed + across_pix(summed, 2)
    input_beside, dy_beside, dy_low, summed = tie(
        beside_rows(messages), dy_beside, dy_low, summed
    )
    summed = pix_sum(summed, 4)
    a_one, stats_one = norm(inputs, totals, *input_beside, rows, gain[0], shift[0])
    one_blocks, kernel_one, two_local, summed = tie(
        gather_blocks(a_one), kernel_one, two_local, summed
    )
    embed_terms = summed[:crop_count]
    ckey = summed[crop_count:, :width].astype(BF)
    cval = summed[crop_count:, width:].astype(BF)
    kernel_two = gather_rows(two_local)
    c_one, totals, *messages = convolve(one_blocks, ids, kernel_one, rows, same, ())
    growth = 1.0 + small(member, embed_terms[:, :width] + offsets[2])
    shift_add = small(member, embed_terms[:, width:] + offsets[3])
    mixed = (growth, shift_add)
    c_beside = beside_rows(messages)
    a_two, stats_two = norm(c_one, totals, *c_beside, rows, gain[1], shift[1], mixed)
    two_blocks, kernel_two, four = tie(gather_blocks(a_two), kernel_two, four)
    four = gather_rows(four)
    resid, totals, *messages = convolve(
        two_blocks, ids, kernel_two, rows, same, (inputs, offsets[0:1])
    )
    resid_beside = beside_rows(messages)
    n_three, stats_three = norm(
        resid, totals, *resid_beside, rows, gain[2], shift[2], active=None, wide=False
    )
    dy_low, n_three, one_blocks, two_blocks = tie(dy_low, n_three, one_blocks, two_blocks)
    three_blocks = gather_blocks(n_three)
    if paired():
        sent = [halves_to_send(blocks, side) for blocks in (one_blocks, two_blocks)]
        three_blocks, sent = tie(three_blocks, sent)
    dy_blocks = gather_blocks(dy_low)
    qkv, head_rows, tail_rows = project(three_blocks, ids, four, 0, 3 * width, edges=True)
    first_dy, qkv = lax.optimization_barrier((dy_blocks[0], qkv))
    datt = project([first_dy] + dy_blocks[1:], ids, four, 3 * width, width)
    low, high = along_pix(tail_rows, 1), along_pix(head_rows, -1)
    if paired():
        low, high, sent = tie(low, high, sent)
        sent, qkv, datt = tie(sent, qkv, datt)
        sent = [across_pix(part, 1) for part in sent]
    chips = jnp.concatenate([home[:1], away])
    found = attend(qkv, datt, low, high, ckey, cval, four, chips, tables)
    if paired():
        found, sent = tie(found, sent)
        one_pairs, two_pairs = [(part, to_mate(part)) for part in sent]
    *parts, att, dquery, dlow, down, dhigh, dckey, dcval = found
    from_prev, from_next = along_pix(dhigh, 1), along_pix(dlow, -1)
    arrived = sent_sums(chip_sums(parts[2:]))
    result = resid + offsets[1:2]
    for piece in home_parts(parts[:2]) + arrived:
        result = result + piece.astype(F32)
    result = pack_rows(result)
    from_prev, from_next, result, att = tie(from_prev, from_next, result, att)
    gap = ((0, tokens - HALO), (0, 0)), ((tokens - HALO, 0), (0, 0))
    down = down + jnp.pad(from_prev.astype(F32), gap[0]) + jnp.pad(from_next.astype(F32), gap[1])
    dqkv = jnp.concatenate([dquery, down.astype(BF)], axis=1)
    sums_three = chip_sums(spread(dqkv, away, four))
    dqkv, sums_three = tie(dqkv, sums_three)
    arrived = sent_sums(sums_three)
    *parts, dmap_three = home_and_outer(dqkv, home_ids, four, three_blocks)
    dmaps = jnp.concatenate([dmap_three, outer(dy_blocks, ids, att)], axis=1)
    parts, arrived, dmaps = tie(parts, arrived, dmaps)
    parts = home_parts(parts) + arrived
    dmaps = scatter_rows(dmaps)
    e_three, raw_three, totals, *messages = gradient_sums(
        parts, resid, stats_three, gain[2], shift[2], same
    )
    e_beside = beside_rows(messages)
    dresid, taps_two, wide_two, *parts = gradient_taps(
        e_three, resid, resid_beside, stats_three, totals, *e_beside, rows, gain[2],
        (dy_low, *dy_beside), away, kernel_two,
    )
    sums_two = chip_sums(parts)
    taps_two, sums_two = tie(taps_two, sums_two)
    arrived = sent_sums(sums_two)
    *parts, dkernel_two = home_and_outer(
        taps_two, home_ids, kernel_two, two_blocks, paired(), shift=W
    )
    if paired():
        beside_two = across_pix(wide_two, 1)
    parts, arrived, dkernel_two = tie(parts, arrived, dkernel_two)
    parts = home_parts(parts) + arrived
    e_two, raw_two, totals, *messages = gradient_sums(
        parts, c_one, stats_two, gain[1], shift[1], same, mixed
    )
    messages, dkernel_two = tie(messages, dkernel_two)
    if paired():
        dkernel_two = half_beside(two_pairs, home_ids[2:], beside_two, other_rows, dkernel_two)
    e_beside, dkernel_two, dmaps = tie(beside_rows(messages), dkernel_two, dmaps)
    dkernel_two = scatter_lines(dkernel_two) if paired() else scatter_rows(dkernel_two)
    taps_one, wide_one, *parts = gradient_taps(
        e_two, c_one, c_beside, stats_two, totals, *e_beside, rows, gain[1], None, away, kernel_one
    )
    sums_one = chip_sums(parts)
    taps_one, sums_one = tie(taps_one, sums_one)
    arrived = sent_sums(sums_one)
    *parts, dkernel_one = home_and_outer(
        taps_one, home_ids, kernel_one, one_blocks, paired(), shift=W
    )
    if paired():
        beside_one = across_pix(wide_one, 1)
        dkernel_one = half_beside(one_pairs, home_ids[2:], beside_one, other_rows, dkernel_one)
    parts, arrived, dkernel_one = tie(parts, arrived, dkernel_one)
    parts = home_parts(parts) + arrived
    demb = jnp.concatenate(
        [turned(member, raw_two[1] * gain[1] + raw_two[0] * shift[1]), turned(member, raw_two[0])]
    )
    e_one, raw_one, totals, *messages = gradient_sums(
        parts, inputs, stats_one, gain[0], shift[0], same, active="plain"
    )
    messages, dkernel_one, dkernel_two = tie(messages, dkernel_one, dkernel_two)
    dkernel_one = scatter_lines(dkernel_one) if paired() else scatter_rows(dkernel_one)
    sums = jnp.concatenate(
        [
            raw_one[1].sum(0)[None],
            (raw_two[1] * growth).sum(0)[None],
            raw_three[1].sum(0)[None],
            raw_one[0].sum(0)[None],
            (raw_two[0] * growth).sum(0)[None],
            raw_three[0].sum(0)[None],
            dresid.sum(0)[None],
            dy_low.astype(F32).sum(0)[None],
            demb,
            dckey,
            dcval,
        ],
        axis=0,
    )
    sums = sums + across_pix(sums, 1)
    e_beside, sums = tie(beside_rows(messages), sums)
    grad_pixels = last_gradient(
        e_one, inputs, stats_one, totals, *e_beside, rows, gain[0], dresid
    )
    sums = sums + across_pix(sums, 2)
    grad_pixels, sums = tie(pack_rows(grad_pixels), sums)
    sums = pix_sum(sums, 4)
    grad_gains, grad_shifts = sums[0:3], sums[3:6]
    demb = sums[8 : 8 + 2 * crop_count].reshape(2, crop_count, width)
    grad_offsets = jnp.concatenate([sums[6:8], demb.sum(1)])
    dcontext = sums[8 + 2 * crop_count :].reshape(2, crop_count * CTX, width)
    own_condition = condition_own.astype(F32)
    grad_embedding = jnp.stack([turned(own_condition, demb[i]) for i in range(2)], axis=2)
    own_context = context_own.astype(F32)
    dcontext_maps = [turned(own_context, dcontext[i]) for i in range(2)]
    dmaps = dmaps.astype(F32).reshape(depth_here, 4, width)
    grad_attention = jnp.stack(
        [dmaps[:, 0], dmaps[:, 1], dmaps[:, 2], *dcontext_maps, dmaps[:, 3]], axis=2
    )
    grad_kernels = pack_kernels(dkernel_one, dkernel_two)
    return (
        result,
        grad_pixels,
        grad_kernels,
        grad_attention.reshape(depth_here, 6 * width),
        grad_embedding.reshape(depth_here, 2 * width),
        grad_gains,
        grad_shifts,
        grad_offsets,
    )


def solution(mesh):
    split = P("pix", "ch")
    tall = P(None, "ch")
    return jax.shard_map(
        local,
        mesh=mesh,
        in_specs=(split, split, P(), P(), P(), split, split, split, tall, tall, tall),
        out_specs=(split, split, split, split, split, tall, tall, tall),
        check_vma=False,
    )
```

profile of v0, /device:TPU:0, one launch (start us, length us, event | category | flops | bytes accessed | tf_op | source)
XLA Modules:
  0.0 647.7 jit_solution(14866955870235234833)
XLA Ops:
  12.2 3.0 collective-permute-start
  15.2 3.6 reshape.152
  18.8 3.2 copy.58
  30.0 4.0 reshape.179
  34.0 5.6 copy.53
  39.6 3.4 stats.1
  43.6 5.2 collective-permute-start.5
  52.3 2.7 collective-permute-done.5
  55.1 2.8 collective-permute-done.2.refs_3_
  58.7 3.2 norm.3
  63.4 16.8 %collective-permute-done.7.refs_2_.refs_4_ = bf16[1600,256]{1,0:T(8,128)(2,1)S(1)} collective-permute-done((bf16[1600,256]{1,0:T(8,128)(2,1)}, bf16[1600,256]{1,0:T(8,128)(2,1)S(1)}, u32[]{:S(2)}, u32[]{:S(2)}) %collective-permute-start.7) | collective-permute-done | bytes 819232 | tf_op jit(solution)/shard_map/ppermute | solution.py:971
  80.2 2.9 collective-permute-start.9
  84.2 16.0 %collective-permute-done.9 = f32[80,512]{1,0:T(8,128)S(1)} collective-permute-done((f32[80,512]{1,0:T(8,128)S(1)}, f32[80,512]{1,0:T(8,128)S(1)}, u32[]{:S(2)}, u32[]{:S(2)}) %collective-permute-start.9) | collective-permute-done | bytes 163872 | tf_op jit(solution)/shard_map/ppermute | solution.py:955
  100.3 2.3 all-gather.4.cloned.1.call-done.refs_4_.refs_10_.refs_1_
  104.4 14.1 %convolve.2 = (f32[1536,256]{1,0:T(8,128)}, f32[2,48,256]{2,1,0:T(8,128)}, f32[40,256]{1,0:T(8,128)}, f32[40,256]{1,0:T(8,128)}) custom-call(s32[4]{0:T(128)} %pad_add_fusion.1.ids, bf16[1600,256]{1,0:T(8,128)(2,1)} %get-tuple-element.207.refs_0_.refs_2_, bf16[1600,256]{1,0:T(8,128)(2,1)} %collective-permute-done.6.refs_1_.refs_3_, ...), custom_call_target="tpu_custom_call" | custom-call | flops 7247757312 | bytes 9437184 | tf_op jit(solution)/shard_map/convolve/pallas_call | solution.py:447
  123.5 3.1 collective-permute-done.11.refs_3_
  127.3 3.3 norm.4
  132.0 17.9 %collective-permute-done.13.refs_2_.refs_4_ = bf16[1600,256]{1,0:T(8,128)(2,1)S(1)} collective-permute-done((bf16[1600,256]{1,0:T(8,128)(2,1)}, bf16[1600,256]{1,0:T(8,128)(2,1)S(1)}, u32[]{:S(2)}, u32[]{:S(2)}) %collective-permute-start.13) | collective-permute-done | bytes 819232 | tf_op jit(solution)/shard_map/ppermute | solution.py:971
  152.4 31.5 %all-gather.6.cloned.1.call-done.refs_4_.refs_13_.refs_1_ = bf16[1024,2304]{1,0:T(8,128)(2,1)} async-done(((bf16[128,2304]{1,0:T(8,128)(2,1)}), bf16[1024,2304]{1,0:T(8,128)(2,1)}) %all-gather.6.cloned.1.call-update) | async-done | bytes 4718608 | tf_op jit(solution)/shard_map/all_gather | solution.py:975
  184.1 14.6 %convolve.3 = (f32[1536,256]{1,0:T(8,128)}, f32[2,48,256]{2,1,0:T(8,128)}, f32[40,256]{1,0:T(8,128)}, f32[40,256]{1,0:T(8,128)}) custom-call(s32[4]{0:T(128)} %pad_add_fusion.1.ids, bf16[1600,256]{1,0:T(8,128)(2,1)} %get-tuple-element.209.refs_0_.refs_2_, bf16[1600,256]{1,0:T(8,128)(2,1)} %collective-permute-done.12.refs_1_.refs_3_, ...), custom_call_target="tpu_custom_call" | custom-call | flops 7247757312 | bytes 9437184 | tf_op jit(solution)/shard_map/convolve/pallas_call | solution.py:447
  198.7 2.5 collective-permute-start.15
  203.2 4.1 collective-permute-done.16.refs_3_
  207.9 2.8 norm.5
  213.8 14.6 %collective-permute-done.18.refs_2_.refs_4_ = bf16[1536,256]{1,0:T(8,128)(2,1)} collective-permute-done((bf16[1536,256]{1,0:T(8,128)(2,1)}, bf16[1536,256]{1,0:T(8,128)(2,1)}, u32[]{:S(2)}, u32[]{:S(2)}) %collective-permute-start.18) | collective-permute-done | bytes 786464 | tf_op jit(solution)/shard_map/ppermute | solution.py:971
  231.9 2.5 all-gather.8.cloned.1.call-done.refs_4_.map_ref.refs_0_.refs_1_
  234.4 7.7 %project.2 = (bf16[1536,768]{1,0:T(8,128)(2,1)}, bf16[992,512]{1,0:T(8,128)(2,1)}, bf16[992,512]{1,0:T(8,128)(2,1)}) custom-call(s32[4]{0:T(128)} %pad_add_fusion.1.ids, bf16[1536,256]{1,0:T(8,128)(2,1)} %get-tuple-element.211.refs_0_.refs_2_, bf16[1536,256]{1,0:T(8,128)(2,1)} %collective-permute-done.17.refs_1_.refs_3_, ...), custom_call_target="tpu_custom_call" | custom-call | flops 2415919104 | bytes 3932160 | tf_op jit(solution)/shard_map/project/pallas_call | solution.py:497
  242.1 3.4 collective-permute-start.20
  251.7 5.0 project.3.grad_ref
  256.6 31.9 %collective-permute-done.20.low_ref = bf16[992,512]{1,0:T(8,128)(2,1)} collective-permute-done((bf16[992,512]{1,0:T(8,128)(2,1)}, bf16[992,512]{1,0:T(8,128)(2,1)}, u32[]{:S(2)}, u32[]{:S(2)}) %collective-permute-start.20) | collective-permute-done | bytes 1015840 | tf_op jit(solution)/shard_map/ppermute | solution.py:951
  288.5 2.5 collective-permute-start.25
  295.2 58.0 %attend.1 = (bf16[1,1536,256]{2,1,0:T(8,128)(2,1)}, bf16[1,1536,256]{2,1,0:T(8,128)(2,1)}, bf16[1,1536,256]{2,1,0:T(8,128)(2,1)}, bf16[1,1536,256]{2,1,0:T(8,128...) custom-call(s32[6]{0:T(128)} %get-tuple-element.363.starts, ...), custom_call_target="tpu_custom_call" | custom-call | flops 2013265920 | bytes 7864320 | tf_op jit(solution)/shard_map/attend/pallas_call | solution.py:911
  357.7 13.2 %collective-permute-start.27 = (bf16[992,512]{1,0:T(8,128)(2,1)}, bf16[992,512]{1,0:T(8,128)(2,1)}, u32[]{:S(2)}, u32[]{:S(2)}) collective-permute-start(bf16[992,512]{1,0:T(8,128)(2,1)} %get-tuple-element.243), channel_id=1, source_target_pairs={{0,4},{4,8},{8,12},{12,16},{16,20},{20,24},{24,28},{1,5},{5,9},{9,... | collective-permute-start | bytes 3047432 | tf_op jit(solution)/shard_map/ppermute | solution.py:951
  373.1 3.7 collective-permute-done.31
  377.2 3.9 copy.65
  381.1 6.2 reshape.157
  387.4 26.5 %collective-permute-done.27 = bf16[992,512]{1,0:T(8,128)(2,1)} collective-permute-done((bf16[992,512]{1,0:T(8,128)(2,1)}, bf16[992,512]{1,0:T(8,128)(2,1)}, u32[]{:S(2)}, u32[]{:S(2)}) %collective-permute-start.27) | collective-permute-done | bytes 1015840 | tf_op jit(solution)/shard_map/ppermute | solution.py:951
  417.5 4.8 spread.1
  422.3 2.5 collective-permute-done.32
  428.3 5.4 outer.1
  433.7 8.8 %home_and_outer.3 = (bf16[1,1536,256]{2,1,0:T(8,128)(2,1)}, bf16[1,1536,256]{2,1,0:T(8,128)(2,1)}, bf16[1024,768]{1,0:T(8,128)(2,1)}) custom-call(s32[7]{0:T(128)} %concatenate.40.ids, bf16[1536,768]{1,0:T(8,128)(2,1)} %pad_maximum_fusion.grad_ref.refs_0_, bf16[1024,1024]{1,0:T(8,128)(2,1)} %all-gather.8.cloned.1.call-done.refs_4_.map_ref.refs_0_.refs_1_, ...), custom_call_target="tpu_custom_call" | custom-call | flops 3623878656 | bytes 4718592 | tf_op jit(solution)/shard_map/home_and_outer/pallas_call | solution.py:575
  442.5 3.1 pad_maximum_fusion.1
  445.9 2.2 collective-permute-done.34.refs_1_
  448.9 4.5 gradient_sums.3
  453.4 4.4 collective-permute-start.35
  459.8 4.1 collective-permute-done.36.refs_7_
  464.5 11.1 %gradient_taps.2 = (f32[1536,256]{1,0:T(8,128)}, bf16[1536,2304]{1,0:T(8,128)(2,1)}, bf16[1600,256]{1,0:T(8,128)(2,1)}, bf16[1,1536,256]{2,1,0:T(8,128)(2,1)}, bf16[1,1536,256]{2,1,0:T(8,128)(2,1)}) custom-call(s32[2]{0:T(128)} %pad_add_fusion.2.ids, f32[1536,256]{1,0:T(8,128)} %get-tuple-element.267.refs_0_, ...), custom_call_target="tpu_custom_call" | custom-call | flops 1811939328 | bytes 14155776 | tf_op jit(solution)/shard_map/gradient_taps/pallas_call | solution.py:351
  475.8 2.5 collective-permute-done.37
  481.1 3.0 collective-permute-start.43
  484.2 15.2 %home_and_outer.4 = (bf16[1,1536,256]{2,1,0:T(8,128)(2,1)}, bf16[1,1536,256]{2,1,0:T(8,128)(2,1)}, f32[512,2304]{1,0:T(8,128)}) custom-call(s32[7]{0:T(128)} %concatenate.40.ids, bf16[1536,2304]{1,0:T(8,128)(2,1)} %get-tuple-element.276.refs_0_, bf16[1024,2304]{1,0:T(8,128)(2,1)} %all-gather.6.cloned.1.call-done.refs_4_.refs_13_.refs_1_, ...), custom_call_target="tpu_custom_call" | custom-call | flops 7247757312 | bytes 11796480 | tf_op jit(solution)/shard_map/home_and_outer/pallas_call | solution.py:575
  502.9 5.3 gradient_sums.4
  508.2 5.1 collective-permute-start.40
  515.8 10.2 %half_beside.2 = bf16[512,2304]{1,0:T(8,128)(2,1)} custom-call(s32[5]{0:T(128)} %concatenate.43.ids, bf16[1536,256]{1,0:T(8,128)(2,1)} %copy-done.72, bf16[1536,256]{1,0:T(8,128)(2,1)} %copy-done.73, bf16[1600,256]{1,0:T(8,128)(2,1)} %copy-done.68, f32[3,48,256]{2,1,0:T(8,128)} %broadcast_in_dim.102.refs_3_, f32[512,2304]{1,0:T(8,128)} %get-tuple-element.296.refs_4_), custom_call_target="tpu_custom_call" | custom-call | flops 3623878656 | bytes 14155776 | tf_op jit(solution)/shard_map/half_beside/pallas_call | solution.py:623
  526.6 10.8 %gradient_taps.3 = (bf16[1536,2304]{1,0:T(8,128)(2,1)}, bf16[1600,256]{1,0:T(8,128)(2,1)}, bf16[1,1536,256]{2,1,0:T(8,128)(2,1)}, bf16[1,1536,256]{2,1,0:T(8,128)(2,1)}) custom-call(s32[2]{0:T(128)} %pad_add_fusion.2.ids, f32[1536,256]{1,0:T(8,128)} %get-tuple-element.287.refs_0_, f32[1536,256]{1,0:T(8,128)} %get-tuple-element.189.refs_0_.refs_3_.refs_1_, ...), custom_call_target="tpu_custom_call" | custom-call | flops 1811939328 | bytes 14155776 | tf_op jit(solution)/shard_map/gradient_taps/pallas_call | solution.py:351
  538.0 2.6 collective-permute-start.47
  543.1 15.0 %home_and_outer.5 = (bf16[1,1536,256]{2,1,0:T(8,128)(2,1)}, bf16[1,1536,256]{2,1,0:T(8,128)(2,1)}, f32[512,2304]{1,0:T(8,128)}) custom-call(s32[7]{0:T(128)} %concatenate.40.ids, bf16[1536,2304]{1,0:T(8,128)(2,1)} %get-tuple-element.303.refs_0_, bf16[1024,2304]{1,0:T(8,128)(2,1)} %all-gather.4.cloned.1.call-done.refs_4_.refs_10_.refs_1_, ...), custom_call_target="tpu_custom_call" | custom-call | flops 7247757312 | bytes 11796480 | tf_op jit(solution)/shard_map/home_and_outer/pallas_call | solution.py:575
  560.3 10.3 %half_beside.3 = bf16[512,2304]{1,0:T(8,128)(2,1)} custom-call(s32[5]{0:T(128)} %concatenate.43.ids, bf16[1536,256]{1,0:T(8,128)(2,1)} %copy-done.70, bf16[1536,256]{1,0:T(8,128)(2,1)} %copy-done.74, bf16[1600,256]{1,0:T(8,128)(2,1)} %copy-done.69, f32[3,48,256]{2,1,0:T(8,128)} %broadcast_in_dim.102.refs_3_, f32[512,2304]{1,0:T(8,128)} %get-tuple-element.311.refs_4_), custom_call_target="tpu_custom_call" | custom-call | flops 3623878656 | bytes 14155776 | tf_op jit(solution)/shard_map/half_beside/pallas_call | solution.py:623
  570.6 2.3 collective-permute-done.48.refs_1_
  573.8 5.3 gradient_sums.5
  589.0 3.3 collective-permute-done.50.after_ref
  594.1 4.4 last_gradient.1
  598.5 5.0 copy.66
  603.4 6.1 reshape.159
  609.9 20.8 %collective-permute-done.53 = f32[168,256]{1,0:T(8,128)S(1)} collective-permute-done((f32[168,256]{1,0:T(8,128)S(1)}, f32[168,256]{1,0:T(8,128)S(1)}, u32[]{:S(2)}, u32[]{:S(2)}) %collective-permute-start.53) | collective-permute-done | bytes 172064 | tf_op jit(solution)/shard_map/ppermute | solution.py:955
  635.7 4.9 pack_kernels.1
  (368 shorter events, 101.3 us)
Async XLA Ops:
  7.2 95.5 %all-gather.4.cloned.1.call-start = ((), (), s32[]{:S(2)}) async-start(), calls=%async_computation.3 | async-start | bytes 5308416 | tf_op jit(solution)/shard_map/all_gather | solution.py:975
  10.8 173.1 %all-gather.6.cloned.1.call-start = ((), (), s32[]{:S(2)}) async-start(), calls=%async_computation.4 | async-start | bytes 5308416 | tf_op jit(solution)/shard_map/all_gather | solution.py:975
  12.2 31.4 %collective-permute-start = (f32[80,512]{1,0:T(8,128)S(1)}, f32[80,512]{1,0:T(8,128)S(1)}, u32[]{:S(2)}, u32[]{:S(2)}) collective-permute-start(f32[80,512]{1,0:T(8,128)S(1)} %pad_maximum_fusion.6), channel_id=1, source_target_pairs={{0,4},{4,0},{8,12},{12,8},{16,20},{20,16},{24,28},{28,24},{1,5},{5... | collective-permute-start | bytes 491528 | tf_op jit(solution)/shard_map/ppermute | solution.py:955
  22.0 225.0 %copy-start.2 = (bf16[48,256,32]{1,2,0:T(8,128)(2,1)}, bf16[48,256,32]{1,2,0:T(8,128)(2,1)S(1)}, u32[]{:S(2)}) copy-start(bf16[48,256,32]{1,2,0:T(8,128)(2,1)S(1)} %copy.58) | copy-start | bytes 2359300
  22.1 33.0 %collective-permute-start.3 = (bf16[32,256]{1,0:T(8,128)(2,1)S(1)}, bf16[32,256]{1,0:T(8,128)(2,1)S(1)}, u32[]{:S(2)}, u32[]{:S(2)}) collective-permute-start(bf16[32,256]{1,0:T(8,128)(2,1)S(1)} %get-tuple-element.367), channel_id=1, source_target_pairs={{0,4},{4,8},{8,12},{12,16},{16,20},{20,24},{24,28},{1,5},{5,9},{9,... | collective-permute-start | bytes 49160 | tf_op jit(solution)/shard_map/ppermute | solution.py:951
  23.9 31.1 %collective-permute-start.4 = (bf16[32,256]{1,0:T(8,128)(2,1)S(1)}, bf16[32,256]{1,0:T(8,128)(2,1)S(1)}, u32[]{:S(2)}, u32[]{:S(2)}) collective-permute-start(bf16[32,256]{1,0:T(8,128)(2,1)S(1)} %get-tuple-element.366), channel_id=1, source_target_pairs={{4,0},{8,4},{12,8},{16,12},{20,16},{24,20},{28,24},{5,1},{9,5},{13... | collective-permute-start | bytes 49160 | tf_op jit(solution)/shard_map/ppermute | solution.py:951
  26.7 95.9 %copy-start.47 = (s32[48]{0:T(128)}, s32[48]{0:T(128)S(1)}, u32[]{:S(2)}) copy-start(s32[48]{0:T(128)S(1)} %slice.198) | copy-start | bytes 580
  43.6 11.3 %collective-permute-start.5 = (f32[80,512]{1,0:T(8,128)S(1)}, f32[80,512]{1,0:T(8,128)S(1)}, u32[]{:S(2)}, u32[]{:S(2)}) collective-permute-start(f32[80,512]{1,0:T(8,128)S(1)} %fusion.61), channel_id=1, source_target_pairs={{0,8},{4,12},{8,0},{12,4},{16,24},{20,28},{24,16},{28,20},{1,9},{5... | collective-permute-start | bytes 491528 | tf_op jit(solution)/shard_map/ppermute | solution.py:955
  48.8 6.2 collective-permute-start.1
  50.9 7.0 %collective-permute-start.2 = (f32[40,256]{1,0:T(8,128)}, f32[40,256]{1,0:T(8,128)S(1)}, u32[]{:S(2)}, u32[]{:S(2)}) collective-permute-start(f32[40,256]{1,0:T(8,128)} %get-tuple-element.176), channel_id=1, source_target_pairs={{4,0},{8,4},{12,8},{16,12},{20,16},{24,20},{28,24},{5,1},{9,5},{13... | collective-permute-start | bytes 122888 | tf_op jit(solution)/shard_map/ppermute | solution.py:951
  61.9 18.3 %collective-permute-start.7 = (bf16[1600,256]{1,0:T(8,128)(2,1)}, bf16[1600,256]{1,0:T(8,128)(2,1)S(1)}, u32[]{:S(2)}, u32[]{:S(2)}) collective-permute-start(bf16[1600,256]{1,0:T(8,128)(2,1)} %get-tuple-element.207.refs_0_.refs_2_), channel_id=1, source_target_pairs={{0,2},{1,3},{2,0},{3,1},{4,6},{5,7},{6,4},{7,5},{8,10},{9,11},{10,... | collective-permute-start | bytes 2457608 | tf_op jit(solution)/shard_map/ppermute | solution.py:971
  63.4 36.9 %collective-permute-start.6 = (bf16[1600,256]{1,0:T(8,128)(2,1)}, bf16[1600,256]{1,0:T(8,128)(2,1)}, u32[]{:S(2)}, u32[]{:S(2)}) collective-permute-start(bf16[1600,256]{1,0:T(8,128)(2,1)} %get-tuple-element.207.refs_0_.refs_2_), channel_id=1, source_target_pairs={{0,1},{1,0},{2,3},{3,2},{4,5},{5,4},{6,7},{7,6},{8,9},{9,8},{10,11... | collective-permute-start | bytes 2457608 | tf_op jit(solution)/shard_map/ppermute | solution.py:966
  80.2 20.1 %collective-permute-start.8 = (bf16[1600,256]{1,0:T(8,128)(2,1)S(1)}, bf16[1600,256]{1,0:T(8,128)(2,1)}, u32[]{:S(2)}, u32[]{:S(2)}) collective-permute-start(bf16[1600,256]{1,0:T(8,128)(2,1)S(1)} %collective-permute-done.7.refs_2_.refs_4_), channel_id=1, source_target_pairs={{0,1},{1,0},{2,3},{3,2},{4,5},{5,4},{6,7},{7,6},{8,9},{9,8},{10,11... | collective-permute-start | bytes 2457608 | tf_op jit(solution)/shard_map/ppermute | solution.py:966
  80.2 20.1 %collective-permute-start.9 = (f32[80,512]{1,0:T(8,128)S(1)}, f32[80,512]{1,0:T(8,128)S(1)}, u32[]{:S(2)}, u32[]{:S(2)}) collective-permute-start(f32[80,512]{1,0:T(8,128)S(1)} %add.177), channel_id=1, source_target_pairs={{0,16},{4,20},{8,24},{12,28},{16,0},{20,4},{24,8},{28,12},{1,17},{... | collective-permute-start | bytes 491528 | tf_op jit(solution)/shard_map/ppermute | solution.py:955
  102.7 131.8 %all-gather.8.cloned.1.call-start = ((), (), s32[]{:S(2)}) async-start(), calls=%async_computation.5 | async-start | bytes 2359296 | tf_op jit(solution)/shard_map/all_gather | solution.py:975
  118.5 5.0 collective-permute-start.10
  120.5 6.1 collective-permute-start.11
  130.5 19.4 %collective-permute-start.13 = (bf16[1600,256]{1,0:T(8,128)(2,1)}, bf16[1600,256]{1,0:T(8,128)(2,1)S(1)}, u32[]{:S(2)}, u32[]{:S(2)}) collective-permute-start(bf16[1600,256]{1,0:T(8,128)(2,1)} %get-tuple-element.209.refs_0_.refs_2_), channel_id=1, source_target_pairs={{0,2},{1,3},{2,0},{3,1},{4,6},{5,7},{6,4},{7,5},{8,10},{9,11},{10,... | collective-permute-start | bytes 2457608 | tf_op jit(solution)/shard_map/ppermute | solution.py:971
  132.0 19.0 %collective-permute-start.12 = (bf16[1600,256]{1,0:T(8,128)(2,1)}, bf16[1600,256]{1,0:T(8,128)(2,1)}, u32[]{:S(2)}, u32[]{:S(2)}) collective-permute-start(bf16[1600,256]{1,0:T(8,128)(2,1)} %get-tuple-element.209.refs_0_.refs_2_), channel_id=1, source_target_pairs={{0,1},{1,0},{2,3},{3,2},{4,5},{5,4},{6,7},{7,6},{8,9},{9,8},{10,11... | collective-permute-start | bytes 2457608 | tf_op jit(solution)/shard_map/ppermute | solution.py:966
  149.9 2.5 collective-permute-start.14
  183.9 342.2 %reduce-scatter.4.cloned.1.call-start = ((), (), s32[]{:S(2)}) async-start(), calls=%async_computation.6 | async-start | bytes 2359296 | tf_op jit(solution)/shard_map/reduce_scatter | solution.py:1000
  198.7 4.4 collective-permute-start.15
  201.2 6.1 collective-permute-start.16
  210.7 17.6 %collective-permute-start.18 = (bf16[1536,256]{1,0:T(8,128)(2,1)}, bf16[1536,256]{1,0:T(8,128)(2,1)}, u32[]{:S(2)}, u32[]{:S(2)}) collective-permute-start(bf16[1536,256]{1,0:T(8,128)(2,1)} %get-tuple-element.211.refs_0_.refs_2_), channel_id=1, source_target_pairs={{0,2},{1,3},{2,0},{3,1},{4,6},{5,7},{6,4},{7,5},{8,10},{9,11},{10,... | collective-permute-start | bytes 2359304 | tf_op jit(solution)/shard_map/ppermute | solution.py:971
  212.2 19.7 %collective-permute-start.17 = (bf16[1536,256]{1,0:T(8,128)(2,1)}, bf16[1536,256]{1,0:T(8,128)(2,1)}, u32[]{:S(2)}, u32[]{:S(2)}) collective-permute-start(bf16[1536,256]{1,0:T(8,128)(2,1)} %get-tuple-element.211.refs_0_.refs_2_), channel_id=1, source_target_pairs={{0,1},{1,0},{2,3},{3,2},{4,5},{5,4},{6,7},{7,6},{8,9},{9,8},{10,11... | collective-permute-start | bytes 2359304 | tf_op jit(solution)/shard_map/ppermute | solution.py:966
  228.3 3.6 collective-permute-start.19
  228.4 20.0 %collective-permute-start.23 = (bf16[1536,256]{1,0:T(8,128)(2,1)S(1)}, bf16[1536,256]{1,0:T(8,128)(2,1)S(1)}, u32[]{:S(2)}, u32[]{:S(2)}) collective-permute-start(bf16[1536,256]{1,0:T(8,128)(2,1)S(1)} %bitcast.151), channel_id=1, source_target_pairs={{0,2},{1,3},{2,0},{3,1},{4,6},{5,7},{6,4},{7,5},{8,10},{9,11},{10,... | collective-permute-start | bytes 2359304 | tf_op jit(solution)/shard_map/ppermute | solution.py:971
  242.1 46.4 %collective-permute-start.20 = (bf16[992,512]{1,0:T(8,128)(2,1)}, bf16[992,512]{1,0:T(8,128)(2,1)}, u32[]{:S(2)}, u32[]{:S(2)}) collective-permute-start(bf16[992,512]{1,0:T(8,128)(2,1)} %get-tuple-element.216), channel_id=1, source_target_pairs={{0,4},{4,8},{8,12},{12,16},{16,20},{20,24},{24,28},{1,5},{5,9},{9,... | collective-permute-start | bytes 3047432 | tf_op jit(solution)/shard_map/ppermute | solution.py:951
  245.6 43.0 %collective-permute-start.21 = (bf16[992,512]{1,0:T(8,128)(2,1)}, bf16[992,512]{1,0:T(8,128)(2,1)}, u32[]{:S(2)}, u32[]{:S(2)}) collective-permute-start(bf16[992,512]{1,0:T(8,128)(2,1)} %get-tuple-element.217), channel_id=1, source_target_pairs={{4,0},{8,4},{12,8},{16,12},{20,16},{24,20},{28,24},{5,1},{9,5},{13... | collective-permute-start | bytes 3047432 | tf_op jit(solution)/shard_map/ppermute | solution.py:951
  247.1 2.4 collective-permute-start.22
  248.4 2.3 collective-permute-start.24
  248.5 42.7 %copy-start.48 = (s32[48]{0:T(128)S(1)}, s32[48]{0:T(128)}, u32[]{:S(2)}) copy-start(s32[48]{0:T(128)} %copy-done.47) | copy-start | bytes 580
  248.5 43.6 %copy-start.51 = (s32[110]{0:T(128)S(1)}, s32[110]{0:T(128)}, u32[]{:S(2)}) copy-start(s32[110]{0:T(128)} %copy-done.50) | copy-start | bytes 1324
  288.5 64.6 %collective-permute-start.25 = (bf16[1536,256]{1,0:T(8,128)(2,1)}, bf16[1536,256]{1,0:T(8,128)(2,1)S(1)}, u32[]{:S(2)}, u32[]{:S(2)}) collective-permute-start(bf16[1536,256]{1,0:T(8,128)(2,1)} %pad_maximum_fusion.2), channel_id=1, source_target_pairs={{0,4},{4,0},{8,12},{12,8},{16,20},{20,16},{24,28},{28,24},{1,5},{5... | collective-permute-start | bytes 2359304 | tf_op jit(solution)/shard_map/ppermute | solution.py:955
  291.0 62.2 %collective-permute-start.26 = (bf16[1536,256]{1,0:T(8,128)(2,1)}, bf16[1536,256]{1,0:T(8,128)(2,1)S(1)}, u32[]{:S(2)}, u32[]{:S(2)}) collective-permute-start(bf16[1536,256]{1,0:T(8,128)(2,1)} %pad_maximum_fusion.3), channel_id=1, source_target_pairs={{0,4},{4,0},{8,12},{12,8},{16,20},{20,16},{24,28},{28,24},{1,5},{5... | collective-permute-start | bytes 2359304 | tf_op jit(solution)/shard_map/ppermute | solution.py:955
  353.2 2.6 collective-permute-start.30
  353.3 19.8 %collective-permute-start.29 = (bf16[1536,256]{1,0:T(8,128)(2,1)}, bf16[1536,256]{1,0:T(8,128)(2,1)S(1)}, u32[]{:S(2)}, u32[]{:S(2)}) collective-permute-start(bf16[1536,256]{1,0:T(8,128)(2,1)} %bitcast.185), channel_id=1, source_target_pairs={{0,1},{1,0},{2,3},{3,2},{4,5},{5,4},{6,7},{7,6},{8,9},{9,8},{10,11... | collective-permute-start | bytes 2359304 | tf_op jit(solution)/shard_map/ppermute | solution.py:966
  357.1 19.6 %collective-permute-start.31 = (bf16[1536,256]{1,0:T(8,128)(2,1)S(1)}, bf16[1536,256]{1,0:T(8,128)(2,1)S(1)}, u32[]{:S(2)}, u32[]{:S(2)}) collective-permute-start(bf16[1536,256]{1,0:T(8,128)(2,1)S(1)} %fusion.3), channel_id=1, source_target_pairs={{0,2},{1,3},{2,0},{3,1},{4,6},{5,7},{6,4},{7,5},{8,10},{9,11},{10,... | collective-permute-start | bytes 2359304 | tf_op jit(solution)/shard_map/ppermute | solution.py:971
  357.7 56.1 %collective-permute-start.27 = (bf16[992,512]{1,0:T(8,128)(2,1)}, bf16[992,512]{1,0:T(8,128)(2,1)}, u32[]{:S(2)}, u32[]{:S(2)}) collective-permute-start(bf16[992,512]{1,0:T(8,128)(2,1)} %get-tuple-element.243), channel_id=1, source_target_pairs={{0,4},{4,8},{8,12},{12,16},{16,20},{20,24},{24,28},{1,5},{5,9},{9,... | collective-permute-start | bytes 3047432 | tf_op jit(solution)/shard_map/ppermute | solution.py:951
  371.0 42.8 %collective-permute-start.28 = (bf16[992,512]{1,0:T(8,128)(2,1)}, bf16[992,512]{1,0:T(8,128)(2,1)}, u32[]{:S(2)}, u32[]{:S(2)}) collective-permute-start(bf16[992,512]{1,0:T(8,128)(2,1)} %get-tuple-element.244), channel_id=1, source_target_pairs={{4,0},{8,4},{12,8},{16,12},{20,16},{24,20},{28,24},{5,1},{9,5},{13... | collective-permute-start | bytes 3047432 | tf_op jit(solution)/shard_map/ppermute | solution.py:951
  422.3 2.5 collective-permute-start.32
  426.1 19.6 %collective-permute-start.33 = (bf16[1536,256]{1,0:T(8,128)(2,1)S(1)}, bf16[1536,256]{1,0:T(8,128)(2,1)S(1)}, u32[]{:S(2)}, u32[]{:S(2)}) collective-permute-start(bf16[1536,256]{1,0:T(8,128)(2,1)S(1)} %fusion.2), channel_id=1, source_target_pairs={{0,2},{1,3},{2,0},{3,1},{4,6},{5,7},{6,4},{7,5},{8,10},{9,11},{10,... | collective-permute-start | bytes 2359304 | tf_op jit(solution)/shard_map/ppermute | solution.py:971
  445.8 2.3 collective-permute-start.34
  445.8 133.3 %reduce-scatter.6.cloned.1.call-start = ((), (), s32[]{:S(2)}) async-start(), calls=%async_computation.7 | async-start | bytes 2949120 | tf_op jit(solution)/shard_map/reduce_scatter | solution.py:985
  453.4 6.4 collective-permute-start.35
  457.8 6.1 collective-permute-start.36
  475.7 2.6 collective-permute-start.37
  479.6 19.8 %collective-permute-start.38 = (bf16[1536,256]{1,0:T(8,128)(2,1)S(1)}, bf16[1536,256]{1,0:T(8,128)(2,1)S(1)}, u32[]{:S(2)}, u32[]{:S(2)}) collective-permute-start(bf16[1536,256]{1,0:T(8,128)(2,1)S(1)} %fusion.1), channel_id=1, source_target_pairs={{0,2},{1,3},{2,0},{3,1},{4,6},{5,7},{6,4},{7,5},{8,10},{9,11},{10,... | collective-permute-start | bytes 2359304 | tf_op jit(solution)/shard_map/ppermute | solution.py:971
  481.1 33.5 %collective-permute-start.43 = (bf16[1600,256]{1,0:T(8,128)(2,1)S(1)}, bf16[1600,256]{1,0:T(8,128)(2,1)S(1)}, u32[]{:S(2)}, u32[]{:S(2)}) collective-permute-start(bf16[1600,256]{1,0:T(8,128)(2,1)S(1)} %copy-done.67), channel_id=1, source_target_pairs={{0,4},{4,0},{8,12},{12,8},{16,20},{20,16},{24,28},{28,24},{1,5},{5... | collective-permute-start | bytes 2457608 | tf_op jit(solution)/shard_map/ppermute | solution.py:955
  499.4 2.6 collective-permute-start.39
  500.2 14.5 %collective-permute-start.42 = (bf16[1536,256]{1,0:T(8,128)(2,1)}, bf16[1536,256]{1,0:T(8,128)(2,1)S(1)}, u32[]{:S(2)}, u32[]{:S(2)}) collective-permute-start(bf16[1536,256]{1,0:T(8,128)(2,1)} %copy-done.72), channel_id=1, source_target_pairs={{0,1},{1,0},{2,3},{3,2},{4,5},{5,4},{6,7},{7,6},{8,9},{9,8},{10,11... | collective-permute-start | bytes 2359304 | tf_op jit(solution)/shard_map/ppermute | solution.py:966
  508.2 17.8 %collective-permute-start.40 = (f32[40,256]{1,0:T(8,128)}, f32[40,256]{1,0:T(8,128)S(1)}, u32[]{:S(2)}, u32[]{:S(2)}) collective-permute-start(f32[40,256]{1,0:T(8,128)} %get-tuple-element.292), channel_id=1, source_target_pairs={{0,4},{4,8},{8,12},{12,16},{16,20},{20,24},{24,28},{1,5},{5,9},{9,... | collective-permute-start | bytes 122888 | tf_op jit(solution)/shard_map/ppermute | solution.py:951
  513.3 12.7 %collective-permute-start.41 = (f32[40,256]{1,0:T(8,128)}, f32[40,256]{1,0:T(8,128)S(1)}, u32[]{:S(2)}, u32[]{:S(2)}) collective-permute-start(f32[40,256]{1,0:T(8,128)} %get-tuple-element.293), channel_id=1, source_target_pairs={{4,0},{8,4},{12,8},{16,12},{20,16},{24,20},{28,24},{5,1},{9,5},{13... | collective-permute-start | bytes 122888 | tf_op jit(solution)/shard_map/ppermute | solution.py:951
  526.1 109.7 %reduce-scatter.8.cloned.1.call-start = ((), (), s32[]{:S(2)}) async-start(), calls=%async_computation.8 | async-start | bytes 2949120 | tf_op jit(solution)/shard_map/reduce_scatter | solution.py:985
  537.4 3.2 collective-permute-start.44
  537.5 20.7 %collective-permute-start.46 = (bf16[1536,256]{1,0:T(8,128)(2,1)S(1)}, bf16[1536,256]{1,0:T(8,128)(2,1)S(1)}, u32[]{:S(2)}, u32[]{:S(2)}) collective-permute-start(bf16[1536,256]{1,0:T(8,128)(2,1)S(1)} %copy-done.71), channel_id=1, source_target_pairs={{0,1},{1,0},{2,3},{3,2},{4,5},{5,4},{6,7},{7,6},{8,9},{9,8},{10,11... | collective-permute-start | bytes 2359304 | tf_op jit(solution)/shard_map/ppermute | solution.py:966
  538.0 21.3 %collective-permute-start.47 = (bf16[1600,256]{1,0:T(8,128)(2,1)}, bf16[1600,256]{1,0:T(8,128)(2,1)S(1)}, u32[]{:S(2)}, u32[]{:S(2)}) collective-permute-start(bf16[1600,256]{1,0:T(8,128)(2,1)} %get-tuple-element.310), channel_id=1, source_target_pairs={{0,4},{4,0},{8,12},{12,8},{16,20},{20,16},{24,28},{28,24},{1,5},{5... | collective-permute-start | bytes 2457608 | tf_op jit(solution)/shard_map/ppermute | solution.py:955
  541.9 28.6 %collective-permute-start.45 = (bf16[1536,256]{1,0:T(8,128)(2,1)S(1)}, bf16[1536,256]{1,0:T(8,128)(2,1)S(1)}, u32[]{:S(2)}, u32[]{:S(2)}) collective-permute-start(bf16[1536,256]{1,0:T(8,128)(2,1)S(1)} %fusion), channel_id=1, source_target_pairs={{0,2},{1,3},{2,0},{3,1},{4,6},{5,7},{6,4},{7,5},{8,10},{9,11},{10,... | collective-permute-start | bytes 2359304 | tf_op jit(solution)/shard_map/ppermute | solution.py:971
  570.5 2.4 collective-permute-start.48
  582.3 6.5 %collective-permute-start.51 = (f32[168,256]{1,0:T(8,128)S(1)}, f32[168,256]{1,0:T(8,128)S(1)}, u32[]{:S(2)}, u32[]{:S(2)}) collective-permute-start(f32[168,256]{1,0:T(8,128)S(1)} %concatenate.44), channel_id=1, source_target_pairs={{0,4},{4,0},{8,12},{12,8},{16,20},{20,16},{24,28},{28,24},{1,5},{5... | collective-permute-start | bytes 516104 | tf_op jit(solution)/shard_map/ppermute | solution.py:955
  584.1 4.8 collective-permute-start.49
  586.3 5.9 collective-permute-start.50
  592.2 17.3 %collective-permute-start.52 = (f32[168,256]{1,0:T(8,128)S(1)}, f32[168,256]{1,0:T(8,128)S(1)}, u32[]{:S(2)}, u32[]{:S(2)}) collective-permute-start(f32[168,256]{1,0:T(8,128)S(1)} %add.206), channel_id=1, source_target_pairs={{0,8},{4,12},{8,0},{12,4},{16,24},{20,28},{24,16},{28,20},{1,9},{5... | collective-permute-start | bytes 516104 | tf_op jit(solution)/shard_map/ppermute | solution.py:955
  609.6 21.1 %collective-permute-start.53 = (f32[168,256]{1,0:T(8,128)S(1)}, f32[168,256]{1,0:T(8,128)S(1)}, u32[]{:S(2)}, u32[]{:S(2)}) collective-permute-start(f32[168,256]{1,0:T(8,128)S(1)} %add.207), channel_id=1, source_target_pairs={{0,16},{4,20},{8,24},{12,28},{16,0},{20,4},{24,8},{28,12},{1,17},{... | collective-permute-start | bytes 516104 | tf_op jit(solution)/shard_map/ppermute | solution.py:955
  (75 other events, 702.9 us)
Sparse Core Ops, SparseCore 0:
  10.9 91.7 all-gather.3
  105.4 78.3 all-gather.5
  186.6 47.8 all-gather.7
  445.9 68.8 reduce-scatter.3
  526.2 47.0 reduce-scatter.5
  579.3 54.1 reduce-scatter.7
where the time goes:
time: 654 us; the launch traced here: 648 us
  Pallas kernels  228 us (35%)
  waiting for transfers between devices  225 us (34%)
  starting transfers between devices  86.1 us (13%)
  local copies, waits for them, and re-layouts  66.2 us (10%)
  other arithmetic  23 us (4%)
  between operations  15.5 us (2%)
    ppermute x18, waiting for transfers between devices, along_pix(): lax.ppermute(value, 'pix', [(i, i + by) for i in range(size) if 0 <= i +...  76.8 us
    pallas_call x1, Pallas kernels, attend(): pl.pallas_call(functools.partial(attention_body, heads), out_shape=(*part...  58 us
    ppermute x8, waiting for transfers between devices, to_chip(): lax.ppermute(value, 'ch', [(i, (i + 2 * by) % size) for i in range(size)])  54.4 us
    ppermute x18, starting transfers between devices, along_pix(): lax.ppermute(value, 'pix', [(i, i + by) for i in range(size) if 0 <= i +...  49.2 us
    ppermute x10, waiting for transfers between devices, across_pix(): lax.ppermute(value, 'pix', [(i, i ^ bit) for i in range(lax.axis_size('pi...  41.9 us
    pallas_call x3, Pallas kernels, home_and_outer(): pl.pallas_call(functools.partial(home_body, count, halved, shift), out_sh...  39 us
    all_gather x3, waiting for transfers between devices, gather_rows(): return lax.all_gather(value, 'pix', axis=0, tiled=True)  36.3 us
    pallas_call x2, Pallas kernels, convolve(): pl.pallas_call(functools.partial(conv_body, count, len(resid)), out_shape...  28.7 us
  transfers between devices with their start and end apart: 60, of which 33 were waited for; matrix products, arithmetic and copies ran while one was open for 12% of the time, Pallas kernels for 34%

commit v1 on v0

--- a/solution.py
+++ b/solution.py
@@ -14,7 +14,7 @@
 GSIZE = 32
 HALO = (CROP_ROWS - 1) * W
 QB = 256
-KB = 256
+KB = 512
 
 HIGHEST = lax.Precision.HIGHEST
 EPSILON = 1e-05
@@ -1189,21 +1189,21 @@
     )
     summed = pix_sum(summed, 4)
     a_one, stats_one = norm(inputs, totals, *input_beside, rows, gain[0], shift[0])
-    one_blocks, kernel_one, two_local, summed = tie(
-        gather_blocks(a_one), kernel_one, two_local, summed
-    )
+    a_one, two_local = tie(a_one, two_local)
+    kernel_two = gather_rows(two_local)
+    one_blocks, kernel_one, summed = tie(gather_blocks(a_one), kernel_one, summed)
     embed_terms = summed[:crop_count]
     ckey = summed[crop_count:, :width].astype(BF)
     cval = summed[crop_count:, width:].astype(BF)
-    kernel_two = gather_rows(two_local)
     c_one, totals, *messages = convolve(one_blocks, ids, kernel_one, rows, same, ())
     growth = 1.0 + small(member, embed_terms[:, :width] + offsets[2])
     shift_add = small(member, embed_terms[:, width:] + offsets[3])
     mixed = (growth, shift_add)
     c_beside = beside_rows(messages)
     a_two, stats_two = norm(c_one, totals, *c_beside, rows, gain[1], shift[1], mixed)
-    two_blocks, kernel_two, four = tie(gather_blocks(a_two), kernel_two, four)
+    a_two, four = tie(a_two, four)
     four = gather_rows(four)
+    two_blocks, kernel_two = tie(gather_blocks(a_two), kernel_two)
     resid, totals, *messages = convolve(
         two_blocks, ids, kernel_two, rows, same, (inputs, offsets[0:1])
     )

time: 654 us -> 647 us (0.989)
    unnamed x169 -> x171, local copies, waits for them, and re-layouts: 14.6 us -> 15.5 us
  transfers between devices with their start and end apart: 60 -> 60, of which waited for: 33 -> 33; matrix products, arithmetic and copies ran while one was open for 12% -> 12% of each run, Pallas kernels for 34% -> 33%
where the time goes in v1:
time: 647 us; the launch traced here: 641 us
  waiting for transfers between devices  224 us (35%)
  Pallas kernels  223 us (34%)
  starting transfers between devices  84.6 us (13%)
  local copies, waits for them, and re-layouts  67.3 us (10%)
  other arithmetic  23.3 us (4%)
  between operations  15.6 us (2%)
    ppermute x18, waiting for transfers between devices, along_pix(): lax.ppermute(value, 'pix', [(i, i + by) for i in range(size) if 0 <= i +...  76.5 us
    ppermute x8, waiting for transfers between devices, to_chip(): lax.ppermute(value, 'ch', [(i, (i + 2 * by) % size) for i in range(size)])  55.6 us
    pallas_call x1, Pallas kernels, attend(): pl.pallas_call(functools.partial(attention_body, heads), out_shape=(*part...  52.9 us
    ppermute x18, starting transfers between devices, along_pix(): lax.ppermute(value, 'pix', [(i, i + by) for i in range(size) if 0 <= i +...  47.1 us
    pallas_call x3, Pallas kernels, home_and_outer(): pl.pallas_call(functools.partial(home_body, count, halved, shift), out_sh...  39 us
    ppermute x10, waiting for transfers between devices, across_pix(): lax.ppermute(value, 'pix', [(i, i ^ bit) for i in range(lax.axis_size('pi...  38.8 us
    all_gather x3, waiting for transfers between devices, gather_rows(): return lax.all_gather(value, 'pix', axis=0, tiled=True)  38.4 us
    pallas_call x2, Pallas kernels, convolve(): pl.pallas_call(functools.partial(conv_body, count, len(resid)), out_shape...  28.7 us
  transfers between devices with their start and end apart: 60, of which 33 were waited for; matrix products, arithmetic and copies ran while one was open for 12% of the time, Pallas kernels for 33%

profile of v1, /device:TPU:0, one launch (start us, length us, event | category | flops | bytes accessed | tf_op | source)
XLA Modules:
  0.0 641.0 jit_solution(13196624366099174577)
XLA Ops:
  12.2 3.0 collective-permute-start
  15.2 3.6 reshape.152
  18.8 3.2 copy.58
  30.2 4.0 reshape.179
  34.3 5.5 copy.53
  39.8 3.4 stats.1
  43.9 5.2 collective-permute-start.5
  49.1 2.0 collective-permute-start.1
  55.3 2.8 collective-permute-done.2.refs_3_
  58.9 3.2 norm.3
  64.4 16.8 %collective-permute-done.7.refs_2_.refs_4_ = bf16[1600,256]{1,0:T(8,128)(2,1)S(1)} collective-permute-done((bf16[1600,256]{1,0:T(8,128)(2,1)}, bf16[1600,256]{1,0:T(8,128)(2,1)S(1)}, u32[]{:S(2)}, u32[]{:S(2)}) %collective-permute-start.7) | collective-permute-done | bytes 819232 | tf_op jit(solution)/shard_map/ppermute | solution.py:971
  81.8 2.9 collective-permute-start.9
  86.3 14.9 %collective-permute-done.9 = f32[80,512]{1,0:T(8,128)S(1)} collective-permute-done((f32[80,512]{1,0:T(8,128)S(1)}, f32[80,512]{1,0:T(8,128)S(1)}, u32[]{:S(2)}, u32[]{:S(2)}) %collective-permute-start.9) | collective-permute-done | bytes 163872 | tf_op jit(solution)/shard_map/ppermute | solution.py:955
  102.6 14.1 %convolve.2 = (f32[1536,256]{1,0:T(8,128)}, f32[2,48,256]{2,1,0:T(8,128)}, f32[40,256]{1,0:T(8,128)}, f32[40,256]{1,0:T(8,128)}) custom-call(s32[4]{0:T(128)} %pad_add_fusion.1.ids, bf16[1600,256]{1,0:T(8,128)(2,1)} %get-tuple-element.211.refs_0_.refs_2_, bf16[1600,256]{1,0:T(8,128)(2,1)} %collective-permute-done.6.refs_1_.refs_3_, ...), custom_call_target="tpu_custom_call" | custom-call | flops 7247757312 | bytes 9437184 | tf_op jit(solution)/shard_map/convolve/pallas_call | solution.py:447
  121.6 3.1 collective-permute-done.11.refs_3_
  125.3 3.3 norm.4
  130.5 17.5 %collective-permute-done.13.refs_2_.refs_4_ = bf16[1600,256]{1,0:T(8,128)(2,1)S(1)} collective-permute-done((bf16[1600,256]{1,0:T(8,128)(2,1)}, bf16[1600,256]{1,0:T(8,128)(2,1)S(1)}, u32[]{:S(2)}, u32[]{:S(2)}) %collective-permute-start.13) | collective-permute-done | bytes 819232 | tf_op jit(solution)/shard_map/ppermute | solution.py:971
  148.0 35.4 %all-gather.6.cloned.1.call-done.refs_4_.refs_13_.refs_1_ = bf16[1024,2304]{1,0:T(8,128)(2,1)} async-done(((bf16[128,2304]{1,0:T(8,128)(2,1)}), bf16[1024,2304]{1,0:T(8,128)(2,1)}) %all-gather.6.cloned.1.call-update) | async-done | bytes 4718608 | tf_op jit(solution)/shard_map/all_gather | solution.py:975
  184.2 14.6 %convolve.3 = (f32[1536,256]{1,0:T(8,128)}, f32[2,48,256]{2,1,0:T(8,128)}, f32[40,256]{1,0:T(8,128)}, f32[40,256]{1,0:T(8,128)}) custom-call(s32[4]{0:T(128)} %pad_add_fusion.1.ids, bf16[1600,256]{1,0:T(8,128)(2,1)} %get-tuple-element.213.refs_0_.refs_2_, bf16[1600,256]{1,0:T(8,128)(2,1)} %copy-done.67, bf16[1600,256]{1,0:T(8,128)(2,1)} %copy-done.25, ...), custom_call_target="tpu_custom_call" | custom-call | flops 7247757312 | bytes 9437184 | tf_op jit(solution)/shard_map/convolve/pallas_call | solution.py:447
  198.9 2.5 collective-permute-start.15
  203.3 4.1 collective-permute-done.16.refs_3_
  208.0 2.8 norm.5
  213.9 14.6 %collective-permute-done.18.refs_2_.refs_4_ = bf16[1536,256]{1,0:T(8,128)(2,1)} collective-permute-done((bf16[1536,256]{1,0:T(8,128)(2,1)}, bf16[1536,256]{1,0:T(8,128)(2,1)}, u32[]{:S(2)}, u32[]{:S(2)}) %collective-permute-start.18) | collective-permute-done | bytes 786464 | tf_op jit(solution)/shard_map/ppermute | solution.py:971
  233.9 7.7 %project.2 = (bf16[1536,768]{1,0:T(8,128)(2,1)}, bf16[992,512]{1,0:T(8,128)(2,1)}, bf16[992,512]{1,0:T(8,128)(2,1)}) custom-call(s32[4]{0:T(128)} %pad_add_fusion.1.ids, bf16[1536,256]{1,0:T(8,128)(2,1)} %get-tuple-element.215.refs_0_.refs_2_, bf16[1536,256]{1,0:T(8,128)(2,1)} %collective-permute-done.17.refs_1_.refs_3_, ...), custom_call_target="tpu_custom_call" | custom-call | flops 2415919104 | bytes 3932160 | tf_op jit(solution)/shard_map/project/pallas_call | solution.py:497
  241.6 3.5 collective-permute-start.20
  251.8 5.0 project.3.grad_ref
  256.8 31.5 %collective-permute-done.20.low_ref = bf16[992,512]{1,0:T(8,128)(2,1)} collective-permute-done((bf16[992,512]{1,0:T(8,128)(2,1)}, bf16[992,512]{1,0:T(8,128)(2,1)}, u32[]{:S(2)}, u32[]{:S(2)}) %collective-permute-start.20) | collective-permute-done | bytes 1015840 | tf_op jit(solution)/shard_map/ppermute | solution.py:951
  288.2 2.5 collective-permute-start.25
  295.0 52.9 %attend.1 = (bf16[1,1536,256]{2,1,0:T(8,128)(2,1)}, bf16[1,1536,256]{2,1,0:T(8,128)(2,1)}, bf16[1,1536,256]{2,1,0:T(8,128)(2,1)}, bf16[1,1536,256]{2,1,0:T(8,128...) custom-call(s32[6]{0:T(128)} %get-tuple-element.367.starts, ...), custom_call_target="tpu_custom_call" | custom-call | flops 2013265920 | bytes 7864320 | tf_op jit(solution)/shard_map/attend/pallas_call | solution.py:911
  352.5 13.4 %collective-permute-start.27 = (bf16[992,512]{1,0:T(8,128)(2,1)}, bf16[992,512]{1,0:T(8,128)(2,1)}, u32[]{:S(2)}, u32[]{:S(2)}) collective-permute-start(bf16[992,512]{1,0:T(8,128)(2,1)} %get-tuple-element.247), channel_id=1, source_target_pairs={{0,4},{4,8},{8,12},{12,16},{16,20},{20,24},{24,28},{1,5},{5,9},{9,... | collective-permute-start | bytes 3047432 | tf_op jit(solution)/shard_map/ppermute | solution.py:951
  368.2 3.4 collective-permute-done.31
  371.9 4.0 copy.65
  375.9 6.2 reshape.157
  382.1 26.6 %collective-permute-done.27 = bf16[992,512]{1,0:T(8,128)(2,1)} collective-permute-done((bf16[992,512]{1,0:T(8,128)(2,1)}, bf16[992,512]{1,0:T(8,128)(2,1)}, u32[]{:S(2)}, u32[]{:S(2)}) %collective-permute-start.27) | collective-permute-done | bytes 1015840 | tf_op jit(solution)/shard_map/ppermute | solution.py:951
  408.7 2.1 add_convert_fusion
  412.4 4.8 spread.1
  417.2 2.5 collective-permute-done.32
  423.2 5.4 outer.1
  428.5 8.8 %home_and_outer.3 = (bf16[1,1536,256]{2,1,0:T(8,128)(2,1)}, bf16[1,1536,256]{2,1,0:T(8,128)(2,1)}, bf16[1024,768]{1,0:T(8,128)(2,1)}) custom-call(s32[7]{0:T(128)} %concatenate.40.ids, bf16[1536,768]{1,0:T(8,128)(2,1)} %pad_maximum_fusion.grad_ref.refs_0_, bf16[1024,1024]{1,0:T(8,128)(2,1)} %all-gather.8.cloned.1.call-done.refs_4_.map_ref.refs_0_.refs_1_, ...), custom_call_target="tpu_custom_call" | custom-call | flops 3623878656 | bytes 4718592 | tf_op jit(solution)/shard_map/home_and_outer/pallas_call | solution.py:575
  437.3 3.1 pad_maximum_fusion.1
  440.7 2.2 collective-permute-done.34.refs_1_
  443.8 4.5 gradient_sums.3
  448.3 4.4 collective-permute-start.35
  454.7 4.1 collective-permute-done.36.refs_7_
  459.4 11.1 %gradient_taps.2 = (f32[1536,256]{1,0:T(8,128)}, bf16[1536,2304]{1,0:T(8,128)(2,1)}, bf16[1600,256]{1,0:T(8,128)(2,1)}, bf16[1,1536,256]{2,1,0:T(8,128)(2,1)}, bf16[1,1536,256]{2,1,0:T(8,128)(2,1)}) custom-call(s32[2]{0:T(128)} %pad_add_fusion.2.ids, f32[1536,256]{1,0:T(8,128)} %get-tuple-element.271.refs_0_, ...), custom_call_target="tpu_custom_call" | custom-call | flops 1811939328 | bytes 14155776 | tf_op jit(solution)/shard_map/gradient_taps/pallas_call | solution.py:351
  470.6 2.5 collective-permute-done.37
  477.6 15.2 %home_and_outer.4 = (bf16[1,1536,256]{2,1,0:T(8,128)(2,1)}, bf16[1,1536,256]{2,1,0:T(8,128)(2,1)}, f32[512,2304]{1,0:T(8,128)}) custom-call(s32[7]{0:T(128)} %concatenate.40.ids, bf16[1536,2304]{1,0:T(8,128)(2,1)} %get-tuple-element.280.refs_0_, bf16[1024,2304]{1,0:T(8,128)(2,1)} %all-gather.6.cloned.1.call-done.refs_4_.refs_13_.refs_1_, ...), custom_call_target="tpu_custom_call" | custom-call | flops 7247757312 | bytes 11796480 | tf_op jit(solution)/shard_map/home_and_outer/pallas_call | solution.py:575
  497.4 5.4 gradient_sums.4
  502.8 3.3 collective-permute-start.40
  508.6 10.2 %half_beside.2 = bf16[512,2304]{1,0:T(8,128)(2,1)} custom-call(s32[5]{0:T(128)} %concatenate.43.ids, bf16[1536,256]{1,0:T(8,128)(2,1)} %copy-done.73, bf16[1536,256]{1,0:T(8,128)(2,1)} %copy-done.74, bf16[1600,256]{1,0:T(8,128)(2,1)} %copy-done.69, f32[3,48,256]{2,1,0:T(8,128)} %broadcast_in_dim.102.refs_3_, f32[512,2304]{1,0:T(8,128)} %get-tuple-element.300.refs_4_), custom_call_target="tpu_custom_call" | custom-call | flops 3623878656 | bytes 14155776 | tf_op jit(solution)/shard_map/half_beside/pallas_call | solution.py:623
  519.5 10.8 %gradient_taps.3 = (bf16[1536,2304]{1,0:T(8,128)(2,1)}, bf16[1600,256]{1,0:T(8,128)(2,1)}, bf16[1,1536,256]{2,1,0:T(8,128)(2,1)}, bf16[1,1536,256]{2,1,0:T(8,128)(2,1)}) custom-call(s32[2]{0:T(128)} %pad_add_fusion.2.ids, f32[1536,256]{1,0:T(8,128)} %get-tuple-element.291.refs_0_, f32[1536,256]{1,0:T(8,128)} %get-tuple-element.192.refs_0_.refs_3_.refs_1_, ...), custom_call_target="tpu_custom_call" | custom-call | flops 1811939328 | bytes 14155776 | tf_op jit(solution)/shard_map/gradient_taps/pallas_call | solution.py:351
  530.8 2.6 collective-permute-start.47
  536.6 15.0 %home_and_outer.5 = (bf16[1,1536,256]{2,1,0:T(8,128)(2,1)}, bf16[1,1536,256]{2,1,0:T(8,128)(2,1)}, f32[512,2304]{1,0:T(8,128)}) custom-call(s32[7]{0:T(128)} %concatenate.40.ids, bf16[1536,2304]{1,0:T(8,128)(2,1)} %get-tuple-element.307.refs_0_, bf16[1024,2304]{1,0:T(8,128)(2,1)} %all-gather.4.cloned.1.call-done.refs_4_.refs_10_.refs_1_, ...), custom_call_target="tpu_custom_call" | custom-call | flops 7247757312 | bytes 11796480 | tf_op jit(solution)/shard_map/home_and_outer/pallas_call | solution.py:575
  553.1 10.3 %half_beside.3 = bf16[512,2304]{1,0:T(8,128)(2,1)} custom-call(s32[5]{0:T(128)} %concatenate.43.ids, bf16[1536,256]{1,0:T(8,128)(2,1)} %copy-done.71, bf16[1536,256]{1,0:T(8,128)(2,1)} %copy-done.75, bf16[1600,256]{1,0:T(8,128)(2,1)} %copy-done.70, f32[3,48,256]{2,1,0:T(8,128)} %broadcast_in_dim.102.refs_3_, f32[512,2304]{1,0:T(8,128)} %get-tuple-element.315.refs_4_), custom_call_target="tpu_custom_call" | custom-call | flops 3623878656 | bytes 14155776 | tf_op jit(solution)/shard_map/half_beside/pallas_call | solution.py:623
  563.5 2.3 collective-permute-done.48.refs_1_
  566.6 5.4 gradient_sums.5
  575.2 2.1 collective-permute-start.51
  582.2 3.0 collective-permute-done.50.after_ref
  585.2 2.4 collective-permute-start.52
  587.6 4.4 last_gradient.1
  592.0 5.0 copy.66
  597.0 6.1 reshape.159
  603.7 20.2 %collective-permute-done.53 = f32[168,256]{1,0:T(8,128)S(1)} collective-permute-done((f32[168,256]{1,0:T(8,128)S(1)}, f32[168,256]{1,0:T(8,128)S(1)}, u32[]{:S(2)}, u32[]{:S(2)}) %collective-permute-start.53) | collective-permute-done | bytes 172064 | tf_op jit(solution)/shard_map/ppermute | solution.py:955
  629.0 4.9 pack_kernels.1
  (370 shorter events, 102.3 us)
Async XLA Ops:
  7.2 95.4 %all-gather.4.cloned.1.call-start = ((), (), s32[]{:S(2)}) async-start(), calls=%async_computation.3 | async-start | bytes 5308416 | tf_op jit(solution)/shard_map/all_gather | solution.py:975
  10.8 172.6 %all-gather.6.cloned.1.call-start = ((), (), s32[]{:S(2)}) async-start(), calls=%async_computation.4 | async-start | bytes 5308416 | tf_op jit(solution)/shard_map/all_gather | solution.py:975
  12.2 31.7 %collective-permute-start = (f32[80,512]{1,0:T(8,128)S(1)}, f32[80,512]{1,0:T(8,128)S(1)}, u32[]{:S(2)}, u32[]{:S(2)}) collective-permute-start(f32[80,512]{1,0:T(8,128)S(1)} %pad_maximum_fusion.6), channel_id=1, source_target_pairs={{0,4},{4,0},{8,12},{12,8},{16,20},{20,16},{24,28},{28,24},{1,5},{5... | collective-permute-start | bytes 491528 | tf_op jit(solution)/shard_map/ppermute | solution.py:955
  22.1 224.5 %copy-start.2 = (bf16[48,256,32]{1,2,0:T(8,128)(2,1)}, bf16[48,256,32]{1,2,0:T(8,128)(2,1)S(1)}, u32[]{:S(2)}) copy-start(bf16[48,256,32]{1,2,0:T(8,128)(2,1)S(1)} %copy.58) | copy-start | bytes 2359300
  22.1 33.2 %collective-permute-start.3 = (bf16[32,256]{1,0:T(8,128)(2,1)S(1)}, bf16[32,256]{1,0:T(8,128)(2,1)S(1)}, u32[]{:S(2)}, u32[]{:S(2)}) collective-permute-start(bf16[32,256]{1,0:T(8,128)(2,1)S(1)} %get-tuple-element.371), channel_id=1, source_target_pairs={{0,4},{4,8},{8,12},{12,16},{16,20},{20,24},{24,28},{1,5},{5,9},{9,... | collective-permute-start | bytes 49160 | tf_op jit(solution)/shard_map/ppermute | solution.py:951
  23.9 31.4 %collective-permute-start.4 = (bf16[32,256]{1,0:T(8,128)(2,1)S(1)}, bf16[32,256]{1,0:T(8,128)(2,1)S(1)}, u32[]{:S(2)}, u32[]{:S(2)}) collective-permute-start(bf16[32,256]{1,0:T(8,128)(2,1)S(1)} %get-tuple-element.370), channel_id=1, source_target_pairs={{4,0},{8,4},{12,8},{16,12},{20,16},{24,20},{28,24},{5,1},{9,5},{13... | collective-permute-start | bytes 49160 | tf_op jit(solution)/shard_map/ppermute | solution.py:951
  27.0 93.8 %copy-start.47 = (s32[48]{0:T(128)}, s32[48]{0:T(128)S(1)}, u32[]{:S(2)}) copy-start(s32[48]{0:T(128)S(1)} %slice.198) | copy-start | bytes 580
  43.9 11.3 %collective-permute-start.5 = (f32[80,512]{1,0:T(8,128)S(1)}, f32[80,512]{1,0:T(8,128)S(1)}, u32[]{:S(2)}, u32[]{:S(2)}) collective-permute-start(f32[80,512]{1,0:T(8,128)S(1)} %fusion.61), channel_id=1, source_target_pairs={{0,8},{4,12},{8,0},{12,4},{16,24},{20,28},{24,16},{28,20},{1,9},{5... | collective-permute-start | bytes 491528 | tf_op jit(solution)/shard_map/ppermute | solution.py:955
  49.1 6.2 collective-permute-start.1
  51.2 7.0 %collective-permute-start.2 = (f32[40,256]{1,0:T(8,128)}, f32[40,256]{1,0:T(8,128)S(1)}, u32[]{:S(2)}, u32[]{:S(2)}) collective-permute-start(f32[40,256]{1,0:T(8,128)} %get-tuple-element.178), channel_id=1, source_target_pairs={{4,0},{8,4},{12,8},{16,12},{20,16},{24,20},{28,24},{5,1},{9,5},{13... | collective-permute-start | bytes 122888 | tf_op jit(solution)/shard_map/ppermute | solution.py:951
  62.2 171.7 %all-gather.8.cloned.1.call-start = ((), (), s32[]{:S(2)}) async-start(), calls=%async_computation.5 | async-start | bytes 2359296 | tf_op jit(solution)/shard_map/all_gather | solution.py:975
  62.8 18.4 %collective-permute-start.7 = (bf16[1600,256]{1,0:T(8,128)(2,1)}, bf16[1600,256]{1,0:T(8,128)(2,1)S(1)}, u32[]{:S(2)}, u32[]{:S(2)}) collective-permute-start(bf16[1600,256]{1,0:T(8,128)(2,1)} %get-tuple-element.211.refs_0_.refs_2_), channel_id=1, source_target_pairs={{0,2},{1,3},{2,0},{3,1},{4,6},{5,7},{6,4},{7,5},{8,10},{9,11},{10,... | collective-permute-start | bytes 2457608 | tf_op jit(solution)/shard_map/ppermute | solution.py:971
  64.4 36.9 %collective-permute-start.6 = (bf16[1600,256]{1,0:T(8,128)(2,1)}, bf16[1600,256]{1,0:T(8,128)(2,1)}, u32[]{:S(2)}, u32[]{:S(2)}) collective-permute-start(bf16[1600,256]{1,0:T(8,128)(2,1)} %get-tuple-element.211.refs_0_.refs_2_), channel_id=1, source_target_pairs={{0,1},{1,0},{2,3},{3,2},{4,5},{5,4},{6,7},{7,6},{8,9},{9,8},{10,11... | collective-permute-start | bytes 2457608 | tf_op jit(solution)/shard_map/ppermute | solution.py:966
  81.2 20.1 %collective-permute-start.8 = (bf16[1600,256]{1,0:T(8,128)(2,1)S(1)}, bf16[1600,256]{1,0:T(8,128)(2,1)}, u32[]{:S(2)}, u32[]{:S(2)}) collective-permute-start(bf16[1600,256]{1,0:T(8,128)(2,1)S(1)} %collective-permute-done.7.refs_2_.refs_4_), channel_id=1, source_target_pairs={{0,1},{1,0},{2,3},{3,2},{4,5},{5,4},{6,7},{7,6},{8,9},{9,8},{10,11... | collective-permute-start | bytes 2457608 | tf_op jit(solution)/shard_map/ppermute | solution.py:966
  81.8 19.5 %collective-permute-start.9 = (f32[80,512]{1,0:T(8,128)S(1)}, f32[80,512]{1,0:T(8,128)S(1)}, u32[]{:S(2)}, u32[]{:S(2)}) collective-permute-start(f32[80,512]{1,0:T(8,128)S(1)} %add.177), channel_id=1, source_target_pairs={{0,16},{4,20},{8,24},{12,28},{16,0},{20,4},{24,8},{28,12},{1,17},{... | collective-permute-start | bytes 491528 | tf_op jit(solution)/shard_map/ppermute | solution.py:955
  116.7 4.9 collective-permute-start.10
  118.6 6.1 collective-permute-start.11
  128.6 19.4 %collective-permute-start.13 = (bf16[1600,256]{1,0:T(8,128)(2,1)}, bf16[1600,256]{1,0:T(8,128)(2,1)S(1)}, u32[]{:S(2)}, u32[]{:S(2)}) collective-permute-start(bf16[1600,256]{1,0:T(8,128)(2,1)} %get-tuple-element.213.refs_0_.refs_2_), channel_id=1, source_target_pairs={{0,2},{1,3},{2,0},{3,1},{4,6},{5,7},{6,4},{7,5},{8,10},{9,11},{10,... | collective-permute-start | bytes 2457608 | tf_op jit(solution)/shard_map/ppermute | solution.py:971
  130.2 388.7 %reduce-scatter.4.cloned.1.call-start = ((), (), s32[]{:S(2)}) async-start(), calls=%async_computation.6 | async-start | bytes 2359296 | tf_op jit(solution)/shard_map/reduce_scatter | solution.py:1000
  130.4 52.9 %collective-permute-start.12 = (bf16[1600,256]{1,0:T(8,128)(2,1)}, bf16[1600,256]{1,0:T(8,128)(2,1)S(1)}, u32[]{:S(2)}, u32[]{:S(2)}) collective-permute-start(bf16[1600,256]{1,0:T(8,128)(2,1)} %get-tuple-element.213.refs_0_.refs_2_), channel_id=1, source_target_pairs={{0,1},{1,0},{2,3},{3,2},{4,5},{5,4},{6,7},{7,6},{8,9},{9,8},{10,11... | collective-permute-start | bytes 2457608 | tf_op jit(solution)/shard_map/ppermute | solution.py:966
  148.0 35.4 %collective-permute-start.14 = (bf16[1600,256]{1,0:T(8,128)(2,1)S(1)}, bf16[1600,256]{1,0:T(8,128)(2,1)}, u32[]{:S(2)}, u32[]{:S(2)}) collective-permute-start(bf16[1600,256]{1,0:T(8,128)(2,1)S(1)} %collective-permute-done.13.refs_2_.refs_4_), channel_id=1, source_target_pairs={{0,1},{1,0},{2,3},{3,2},{4,5},{5,4},{6,7},{7,6},{8,9},{9,8},{10,11... | collective-permute-start | bytes 2457608 | tf_op jit(solution)/shard_map/ppermute | solution.py:966
  198.9 4.4 collective-permute-start.15
  201.3 6.1 collective-permute-start.16
  210.9 17.6 %collective-permute-start.18 = (bf16[1536,256]{1,0:T(8,128)(2,1)}, bf16[1536,256]{1,0:T(8,128)(2,1)}, u32[]{:S(2)}, u32[]{:S(2)}) collective-permute-start(bf16[1536,256]{1,0:T(8,128)(2,1)} %get-tuple-element.215.refs_0_.refs_2_), channel_id=1, source_target_pairs={{0,2},{1,3},{2,0},{3,1},{4,6},{5,7},{6,4},{7,5},{8,10},{9,11},{10,... | collective-permute-start | bytes 2359304 | tf_op jit(solution)/shard_map/ppermute | solution.py:971
  212.4 19.7 %collective-permute-start.17 = (bf16[1536,256]{1,0:T(8,128)(2,1)}, bf16[1536,256]{1,0:T(8,128)(2,1)}, u32[]{:S(2)}, u32[]{:S(2)}) collective-permute-start(bf16[1536,256]{1,0:T(8,128)(2,1)} %get-tuple-element.215.refs_0_.refs_2_), channel_id=1, source_target_pairs={{0,1},{1,0},{2,3},{3,2},{4,5},{5,4},{6,7},{7,6},{8,9},{9,8},{10,11... | collective-permute-start | bytes 2359304 | tf_op jit(solution)/shard_map/ppermute | solution.py:966
  228.5 3.6 collective-permute-start.19
  228.6 20.0 %collective-permute-start.23 = (bf16[1536,256]{1,0:T(8,128)(2,1)S(1)}, bf16[1536,256]{1,0:T(8,128)(2,1)S(1)}, u32[]{:S(2)}, u32[]{:S(2)}) collective-permute-start(bf16[1536,256]{1,0:T(8,128)(2,1)S(1)} %bitcast.151), channel_id=1, source_target_pairs={{0,2},{1,3},{2,0},{3,1},{4,6},{5,7},{6,4},{7,5},{8,10},{9,11},{10,... | collective-permute-start | bytes 2359304 | tf_op jit(solution)/shard_map/ppermute | solution.py:971
  241.6 46.7 %collective-permute-start.20 = (bf16[992,512]{1,0:T(8,128)(2,1)}, bf16[992,512]{1,0:T(8,128)(2,1)}, u32[]{:S(2)}, u32[]{:S(2)}) collective-permute-start(bf16[992,512]{1,0:T(8,128)(2,1)} %get-tuple-element.220), channel_id=1, source_target_pairs={{0,4},{4,8},{8,12},{12,16},{16,20},{20,24},{24,28},{1,5},{5,9},{9,... | collective-permute-start | bytes 3047432 | tf_op jit(solution)/shard_map/ppermute | solution.py:951
  245.0 43.2 %collective-permute-start.21 = (bf16[992,512]{1,0:T(8,128)(2,1)}, bf16[992,512]{1,0:T(8,128)(2,1)}, u32[]{:S(2)}, u32[]{:S(2)}) collective-permute-start(bf16[992,512]{1,0:T(8,128)(2,1)} %get-tuple-element.221), channel_id=1, source_target_pairs={{4,0},{8,4},{12,8},{16,12},{20,16},{24,20},{28,24},{5,1},{9,5},{13... | collective-permute-start | bytes 3047432 | tf_op jit(solution)/shard_map/ppermute | solution.py:951
  246.5 2.4 collective-permute-start.22
  248.6 2.3 collective-permute-start.24
  248.6 42.3 %copy-start.48 = (s32[48]{0:T(128)S(1)}, s32[48]{0:T(128)}, u32[]{:S(2)}) copy-start(s32[48]{0:T(128)} %copy-done.47) | copy-start | bytes 580
  248.6 43.2 %copy-start.51 = (s32[110]{0:T(128)S(1)}, s32[110]{0:T(128)}, u32[]{:S(2)}) copy-start(s32[110]{0:T(128)} %copy-done.50) | copy-start | bytes 1324
  288.2 59.7 %collective-permute-start.25 = (bf16[1536,256]{1,0:T(8,128)(2,1)}, bf16[1536,256]{1,0:T(8,128)(2,1)S(1)}, u32[]{:S(2)}, u32[]{:S(2)}) collective-permute-start(bf16[1536,256]{1,0:T(8,128)(2,1)} %pad_maximum_fusion.2), channel_id=1, source_target_pairs={{0,4},{4,0},{8,12},{12,8},{16,20},{20,16},{24,28},{28,24},{1,5},{5... | collective-permute-start | bytes 2359304 | tf_op jit(solution)/shard_map/ppermute | solution.py:955
  290.7 57.3 %collective-permute-start.26 = (bf16[1536,256]{1,0:T(8,128)(2,1)}, bf16[1536,256]{1,0:T(8,128)(2,1)S(1)}, u32[]{:S(2)}, u32[]{:S(2)}) collective-permute-start(bf16[1536,256]{1,0:T(8,128)(2,1)} %pad_maximum_fusion.3), channel_id=1, source_target_pairs={{0,4},{4,0},{8,12},{12,8},{16,20},{20,16},{24,28},{28,24},{1,5},{5... | collective-permute-start | bytes 2359304 | tf_op jit(solution)/shard_map/ppermute | solution.py:955
  348.0 2.6 collective-permute-start.30
  348.1 20.1 %collective-permute-start.29 = (bf16[1536,256]{1,0:T(8,128)(2,1)}, bf16[1536,256]{1,0:T(8,128)(2,1)S(1)}, u32[]{:S(2)}, u32[]{:S(2)}) collective-permute-start(bf16[1536,256]{1,0:T(8,128)(2,1)} %bitcast.185), channel_id=1, source_target_pairs={{0,1},{1,0},{2,3},{3,2},{4,5},{5,4},{6,7},{7,6},{8,9},{9,8},{10,11... | collective-permute-start | bytes 2359304 | tf_op jit(solution)/shard_map/ppermute | solution.py:966
  351.9 19.6 %collective-permute-start.31 = (bf16[1536,256]{1,0:T(8,128)(2,1)S(1)}, bf16[1536,256]{1,0:T(8,128)(2,1)S(1)}, u32[]{:S(2)}, u32[]{:S(2)}) collective-permute-start(bf16[1536,256]{1,0:T(8,128)(2,1)S(1)} %fusion.3), channel_id=1, source_target_pairs={{0,2},{1,3},{2,0},{3,1},{4,6},{5,7},{6,4},{7,5},{8,10},{9,11},{10,... | collective-permute-start | bytes 2359304 | tf_op jit(solution)/shard_map/ppermute | solution.py:971
  352.5 56.2 %collective-permute-start.27 = (bf16[992,512]{1,0:T(8,128)(2,1)}, bf16[992,512]{1,0:T(8,128)(2,1)}, u32[]{:S(2)}, u32[]{:S(2)}) collective-permute-start(bf16[992,512]{1,0:T(8,128)(2,1)} %get-tuple-element.247), channel_id=1, source_target_pairs={{0,4},{4,8},{8,12},{12,16},{16,20},{20,24},{24,28},{1,5},{5,9},{9,... | collective-permute-start | bytes 3047432 | tf_op jit(solution)/shard_map/ppermute | solution.py:951
  365.9 42.9 %collective-permute-start.28 = (bf16[992,512]{1,0:T(8,128)(2,1)}, bf16[992,512]{1,0:T(8,128)(2,1)}, u32[]{:S(2)}, u32[]{:S(2)}) collective-permute-start(bf16[992,512]{1,0:T(8,128)(2,1)} %get-tuple-element.248), channel_id=1, source_target_pairs={{4,0},{8,4},{12,8},{16,12},{20,16},{24,20},{28,24},{5,1},{9,5},{13... | collective-permute-start | bytes 3047432 | tf_op jit(solution)/shard_map/ppermute | solution.py:951
  417.2 2.5 collective-permute-start.32
  421.0 19.6 %collective-permute-start.33 = (bf16[1536,256]{1,0:T(8,128)(2,1)S(1)}, bf16[1536,256]{1,0:T(8,128)(2,1)S(1)}, u32[]{:S(2)}, u32[]{:S(2)}) collective-permute-start(bf16[1536,256]{1,0:T(8,128)(2,1)S(1)} %fusion.2), channel_id=1, source_target_pairs={{0,2},{1,3},{2,0},{3,1},{4,6},{5,7},{6,4},{7,5},{8,10},{9,11},{10,... | collective-permute-start | bytes 2359304 | tf_op jit(solution)/shard_map/ppermute | solution.py:971
  440.7 2.3 collective-permute-start.34
  440.7 131.3 %reduce-scatter.6.cloned.1.call-start = ((), (), s32[]{:S(2)}) async-start(), calls=%async_computation.7 | async-start | bytes 2949120 | tf_op jit(solution)/shard_map/reduce_scatter | solution.py:985
  448.3 6.4 collective-permute-start.35
  452.7 6.1 collective-permute-start.36
  470.5 2.6 collective-permute-start.37
  474.4 19.6 %collective-permute-start.38 = (bf16[1536,256]{1,0:T(8,128)(2,1)S(1)}, bf16[1536,256]{1,0:T(8,128)(2,1)S(1)}, u32[]{:S(2)}, u32[]{:S(2)}) collective-permute-start(bf16[1536,256]{1,0:T(8,128)(2,1)S(1)} %fusion.1), channel_id=1, source_target_pairs={{0,2},{1,3},{2,0},{3,1},{4,6},{5,7},{6,4},{7,5},{8,10},{9,11},{10,... | collective-permute-start | bytes 2359304 | tf_op jit(solution)/shard_map/ppermute | solution.py:971
  476.0 31.5 %collective-permute-start.43 = (bf16[1600,256]{1,0:T(8,128)(2,1)S(1)}, bf16[1600,256]{1,0:T(8,128)(2,1)S(1)}, u32[]{:S(2)}, u32[]{:S(2)}) collective-permute-start(bf16[1600,256]{1,0:T(8,128)(2,1)S(1)} %copy-done.68), channel_id=1, source_target_pairs={{0,4},{4,0},{8,12},{12,8},{16,20},{20,16},{24,28},{28,24},{1,5},{5... | collective-permute-start | bytes 2457608 | tf_op jit(solution)/shard_map/ppermute | solution.py:955
  494.0 2.5 collective-permute-start.39
  494.7 12.7 %collective-permute-start.42 = (bf16[1536,256]{1,0:T(8,128)(2,1)}, bf16[1536,256]{1,0:T(8,128)(2,1)S(1)}, u32[]{:S(2)}, u32[]{:S(2)}) collective-permute-start(bf16[1536,256]{1,0:T(8,128)(2,1)} %copy-done.73), channel_id=1, source_target_pairs={{0,1},{1,0},{2,3},{3,2},{4,5},{5,4},{6,7},{7,6},{8,9},{9,8},{10,11... | collective-permute-start | bytes 2359304 | tf_op jit(solution)/shard_map/ppermute | solution.py:966
  502.8 16.0 %collective-permute-start.40 = (f32[40,256]{1,0:T(8,128)}, f32[40,256]{1,0:T(8,128)S(1)}, u32[]{:S(2)}, u32[]{:S(2)}) collective-permute-start(f32[40,256]{1,0:T(8,128)} %get-tuple-element.296), channel_id=1, source_target_pairs={{0,4},{4,8},{8,12},{12,16},{16,20},{20,24},{24,28},{1,5},{5,9},{9,... | collective-permute-start | bytes 122888 | tf_op jit(solution)/shard_map/ppermute | solution.py:951
  506.1 12.7 %collective-permute-start.41 = (f32[40,256]{1,0:T(8,128)}, f32[40,256]{1,0:T(8,128)S(1)}, u32[]{:S(2)}, u32[]{:S(2)}) collective-permute-start(f32[40,256]{1,0:T(8,128)} %get-tuple-element.297), channel_id=1, source_target_pairs={{4,0},{8,4},{12,8},{16,12},{20,16},{24,20},{28,24},{5,1},{9,5},{13... | collective-permute-start | bytes 122888 | tf_op jit(solution)/shard_map/ppermute | solution.py:951
  518.9 110.1 %reduce-scatter.8.cloned.1.call-start = ((), (), s32[]{:S(2)}) async-start(), calls=%async_computation.8 | async-start | bytes 2949120 | tf_op jit(solution)/shard_map/reduce_scatter | solution.py:985
  530.3 3.2 collective-permute-start.44
  530.3 21.3 %collective-permute-start.46 = (bf16[1536,256]{1,0:T(8,128)(2,1)S(1)}, bf16[1536,256]{1,0:T(8,128)(2,1)S(1)}, u32[]{:S(2)}, u32[]{:S(2)}) collective-permute-start(bf16[1536,256]{1,0:T(8,128)(2,1)S(1)} %copy-done.72), channel_id=1, source_target_pairs={{0,1},{1,0},{2,3},{3,2},{4,5},{5,4},{6,7},{7,6},{8,9},{9,8},{10,11... | collective-permute-start | bytes 2359304 | tf_op jit(solution)/shard_map/ppermute | solution.py:966
  530.8 21.3 %collective-permute-start.47 = (bf16[1600,256]{1,0:T(8,128)(2,1)}, bf16[1600,256]{1,0:T(8,128)(2,1)S(1)}, u32[]{:S(2)}, u32[]{:S(2)}) collective-permute-start(bf16[1600,256]{1,0:T(8,128)(2,1)} %get-tuple-element.314), channel_id=1, source_target_pairs={{0,4},{4,0},{8,12},{12,8},{16,20},{20,16},{24,28},{28,24},{1,5},{5... | collective-permute-start | bytes 2457608 | tf_op jit(solution)/shard_map/ppermute | solution.py:955
  534.8 28.6 %collective-permute-start.45 = (bf16[1536,256]{1,0:T(8,128)(2,1)S(1)}, bf16[1536,256]{1,0:T(8,128)(2,1)S(1)}, u32[]{:S(2)}, u32[]{:S(2)}) collective-permute-start(bf16[1536,256]{1,0:T(8,128)(2,1)S(1)} %fusion), channel_id=1, source_target_pairs={{0,2},{1,3},{2,0},{3,1},{4,6},{5,7},{6,4},{7,5},{8,10},{9,11},{10,... | collective-permute-start | bytes 2359304 | tf_op jit(solution)/shard_map/ppermute | solution.py:971
  563.4 2.4 collective-permute-start.48
  575.2 6.8 %collective-permute-start.51 = (f32[168,256]{1,0:T(8,128)S(1)}, f32[168,256]{1,0:T(8,128)S(1)}, u32[]{:S(2)}, u32[]{:S(2)}) collective-permute-start(f32[168,256]{1,0:T(8,128)S(1)} %concatenate.44), channel_id=1, source_target_pairs={{0,4},{4,0},{8,12},{12,8},{16,20},{20,16},{24,28},{28,24},{1,5},{5... | collective-permute-start | bytes 516104 | tf_op jit(solution)/shard_map/ppermute | solution.py:955
  577.4 4.8 collective-permute-start.49
  579.3 5.9 collective-permute-start.50
  585.2 17.9 %collective-permute-start.52 = (f32[168,256]{1,0:T(8,128)S(1)}, f32[168,256]{1,0:T(8,128)S(1)}, u32[]{:S(2)}, u32[]{:S(2)}) collective-permute-start(f32[168,256]{1,0:T(8,128)S(1)} %add.206), channel_id=1, source_target_pairs={{0,8},{4,12},{8,0},{12,4},{16,24},{20,28},{24,16},{28,20},{1,9},{5... | collective-permute-start | bytes 516104 | tf_op jit(solution)/shard_map/ppermute | solution.py:955
  603.2 20.8 %collective-permute-start.53 = (f32[168,256]{1,0:T(8,128)S(1)}, f32[168,256]{1,0:T(8,128)S(1)}, u32[]{:S(2)}, u32[]{:S(2)}) collective-permute-start(f32[168,256]{1,0:T(8,128)S(1)} %add.207), channel_id=1, source_target_pairs={{0,16},{4,20},{8,24},{12,28},{16,0},{20,4},{24,8},{28,12},{1,17},{... | collective-permute-start | bytes 516104 | tf_op jit(solution)/shard_map/ppermute | solution.py:955
  (76 other events, 666.9 us)
Sparse Core Ops, SparseCore 0:
  10.9 91.6 all-gather.3
  105.3 77.9 all-gather.5
  186.0 47.7 all-gather.7
  440.8 71.3 reduce-scatter.3
  519.0 47.6 reduce-scatter.5
  572.2 54.7 reduce-scatter.7
